TPU v7x, 512 devices: a whole 4x8x8 slice. The times are simulated.
512 devices in a mesh: group: 16 (over y, x_lo), fsdp: 32 (over x_hi, z, core).
Axes of the slice: x: 4 (x_hi: 2, x_lo: 2; x = x_hi * 2 + x_lo), y: 8, z: 8, core: 2. Of those that a mesh axis runs over, the one named last changes fastest.
Arguments:
- grad_terms: bfloat16 [16, 32, 64, 8192], P('group', 'fsdp'), may hold values from -0.59765625 to 0.59765625
- master: float32 [64, 8192], P('fsdp'), may hold values from -6 to 6
- inner_drift: float32 [16, 64, 8192], P('group', 'fsdp'), may hold values from -0.6 to 0.6
- momentum: float32 [64, 8192], P('fsdp'), may hold values from -3 to 3
- moment_codes: int32 [16, 64, 8192], P('group', 'fsdp'), may hold values from 0 to 255
- second_codes: int32 [16, 64, 8192], P('group', 'fsdp'), may hold values from 0 to 255
- moment_scale: float32 [16, 64, 32], P('group', 'fsdp'), may hold values from 0.01 to 0.1
- second_scale: float32 [16, 64, 32], P('group', 'fsdp'), may hold values from 0.05 to 0.5
- counts: int32 [16], P('group'), may hold values from 256 to 6144, as said below
Outputs:
- master_new: float32 [64, 8192], P('fsdp')
- momentum_new: float32 [64, 8192], P('fsdp')
- moment_new: float32 [16, 64, 8192], P('group', 'fsdp')
- second_new: float32 [16, 64, 8192], P('group', 'fsdp')
- model_copy: bfloat16 [64, 8192], replicated
Inputs may be any that keep to these rules, and one draw needn't show every extreme that they name: `counts`: one group trained on 6144 tokens, every other on 256 to 2048.
All inputs are finite; a program needn't handle non-finite values.
Results may differ from a plain program's by a relative error of at most 0.0004.
Values may be sent and summed in bfloat16 or wider, within the bound.
A program may use at most 64 MiB of HBM per device.

v0:
```python
import jax
import jax.numpy as jnp
from jax import lax
from jax.sharding import PartitionSpec as P

BLOCK = 256
STEP = 500


def blockwise(values, scale):
    shaped = values.reshape(values.shape[:-1] + (values.shape[-1] // BLOCK, BLOCK))
    return (shaped * scale[..., None]).reshape(values.shape)


def nesterov(mean_pseudo, master, momentum):
    momentum_new = 0.9 * momentum + mean_pseudo
    master_new = master - 0.7 * (mean_pseudo + 0.9 * momentum_new)
    return (master_new, momentum_new)


def on_device(
    grad_terms,
    master,
    inner_drift,
    momentum,
    moment_codes,
    second_codes,
    moment_scale,
    second_scale,
    counts,
):
    inner = master + inner_drift[0]
    weight = counts.astype(jnp.float32)[0]
    summed = lax.psum_scatter(
        grad_terms.astype(jnp.float32), "fsdp", scatter_dimension=2, tiled=True
    )
    grad = summed[:, 0]
    signed = (moment_codes.astype(jnp.float32) - 127.5) / 127.5
    moment_old = blockwise(signed * signed * signed, moment_scale)
    unsigned = (second_codes.astype(jnp.float32) + 16.0) / 271.0
    second_old = blockwise(unsigned * unsigned, second_scale)
    moment_new = 0.9 * moment_old + 0.1 * grad
    second_new = 0.999 * second_old + 0.001 * grad * grad
    update = moment_new / (1.0 - 0.9**STEP) / (jnp.sqrt(second_new / (1.0 - 0.999**STEP)) + 1e-08)
    pseudo = master - (inner - 0.8 * (update[0] + 0.025 * inner))
    weighted = weight * pseudo
    total_rows, total_count = lax.psum((weighted, weight), "group")
    master_new, momentum_new = nesterov(total_rows / total_count, master, momentum)
    model_copy = lax.all_gather(master_new.astype(jnp.bfloat16), "fsdp", axis=0, tiled=True)
    return (master_new, momentum_new, moment_new, second_new, model_copy)


def solution(mesh):
    in_specs = (
        P("group", "fsdp", None, None),
        P("fsdp", None),
        P("group", "fsdp", None),
        P("fsdp", None),
        P("group", "fsdp", None),
        P("group", "fsdp", None),
        P("group", "fsdp", None),
        P("group", "fsdp", None),
        P("group"),
    )
    out_specs = (
        P("fsdp", None),
        P("fsdp", None),
        P("group", "fsdp", None),
        P("group", "fsdp", None),
        P(),
    )
    return jax.shard_map(
        on_device, mesh=mesh, in_specs=in_specs, out_specs=out_specs, check_vma=False
    )
```

profile of v0, /device:TPU:1, one launch (start us, length us, event | category | flops | bytes accessed | tf_op | source)
XLA Modules:
  0.0 398.8 jit_solution(11685884509597873997)
XLA Ops:
  7.2 0.0 copy-start.5
  7.2 0.0 copy-start.6
  7.2 0.0 copy-start
  7.2 0.0 copy-start.1
  7.2 0.0 copy-start.3
  7.2 0.0 copy-start.2
  7.2 0.0 all-reduce.4.cloned.1.call-start
  8.0 0.0 copy-start.4
  8.0 157.2 %all-reduce.5 = f32[1,1,64,8192]{3,2,1,0:T(8,128)S(1)} all-reduce(bf16[1,1,64,8192]{3,2,1,0:T(8,128)(2,1)} %param.9), channel_id=2, replica_groups=mesh['group'=16,'fsdp'=32] {'fsdp'}, use_global_device_ids=true, to_apply=%region_0.0.clone | all-reduce | flops 524288 | bytes 3145728
  165.1 0.0 copy-done.5
  165.2 0.1 mul.137
  165.3 0.0 copy-done.6
  165.3 0.1 mul.146
  165.4 1.3 dynamic-slice
  167.3 0.0 copy-done
  167.4 0.0 copy-done.1
  167.4 0.0 copy-done.3
  167.4 0.0 copy-done.2
  167.4 1.0 fusion.7
  168.4 0.0 all-reduce.4.cloned.1.call-update
  168.4 0.0 all-gather.3.cloned.1.call-start
  168.5 28.3 %psum.15 = f32[]{:T(128)} all-reduce(f32[]{:T(128)} %bitcast.2), channel_id=1, replica_groups=mesh['group'=16,'fsdp'=32] {'group'}, use_global_device_ids=true, to_apply=%region_2.0 | all-reduce | flops 1 | bytes 8 | tf_op jit(solution)/shard_map/psum | solution.py:47
  196.8 95.9 %all-reduce.4.cloned.1.call-done = f32[2,8192]{1,0:T(2,128)} async-done(((f32[2,8192]{1,0:T(2,128)}), f32[2,8192]{1,0:T(2,128)}) %all-reduce.4.cloned.1.call-update) | async-done | bytes 65552 | tf_op jit(solution)/shard_map/psum | solution.py:47
  292.7 0.0 copy-done.4
  292.7 2.2 convert_bitcast_fusion
  294.9 0.0 all-gather.3.cloned.1.call-update
  295.0 94.7 %all-gather.3.cloned.1.call-done = bf16[32,2,8192]{2,1,0:T(2,128)(2,1)} async-done(((bf16[1,2,8192]{2,1,0:T(2,128)(2,1)}), bf16[32,2,8192]{2,1,0:T(2,128)(2,1)}) %all-gather.3.cloned.1.call-update) | async-done | bytes 1048592 | tf_op jit(solution)/shard_map/all_gather | solution.py:49
  389.7 2.2 reshape.84
  (2 shorter events, 0.1 us)
Async XLA Ops:
  7.2 158.0 %copy-start.5 = (f32[1,2,32]{2,1,0:T(2,128)S(1)}, f32[1,2,32]{2,1,0:T(2,128)}, u32[]{:S(2)}) copy-start(f32[1,2,32]{2,1,0:T(2,128)} %param.15) | copy-start | bytes 772
  7.2 158.1 %copy-start.6 = (f32[1,2,32]{2,1,0:T(2,128)S(1)}, f32[1,2,32]{2,1,0:T(2,128)}, u32[]{:S(2)}) copy-start(f32[1,2,32]{2,1,0:T(2,128)} %param.16) | copy-start | bytes 772
  7.2 160.2 %copy-start = (f32[2,8192]{1,0:T(2,128)S(1)}, f32[2,8192]{1,0:T(2,128)}, u32[]{:S(2)}) copy-start(f32[2,8192]{1,0:T(2,128)} %param.10) | copy-start | bytes 196612
  7.2 160.2 %copy-start.1 = (f32[1,2,8192]{2,1,0:T(2,128)S(1)}, f32[1,2,8192]{2,1,0:T(2,128)}, u32[]{:S(2)}) copy-start(f32[1,2,8192]{2,1,0:T(2,128)} %param.11) | copy-start | bytes 196612
  7.2 160.2 %copy-start.3 = (s32[1,2,8192]{2,1,0:T(2,128)S(1)}, s32[1,2,8192]{2,1,0:T(2,128)}, u32[]{:S(2)}) copy-start(s32[1,2,8192]{2,1,0:T(2,128)} %param.13) | copy-start | bytes 196612
  7.2 160.2 %copy-start.2 = (s32[1,2,8192]{2,1,0:T(2,128)S(1)}, s32[1,2,8192]{2,1,0:T(2,128)}, u32[]{:S(2)}) copy-start(s32[1,2,8192]{2,1,0:T(2,128)} %param.14) | copy-start | bytes 196612
  7.2 285.5 %all-reduce.4.cloned.1.call-start = ((), (), s32[]{:S(2)}) async-start(), calls=%async_computation | async-start | bytes 131072 | tf_op jit(solution)/shard_map/psum | solution.py:47
  8.0 284.7 %copy-start.4 = (f32[2,8192]{1,0:T(2,128)S(1)}, f32[2,8192]{1,0:T(2,128)}, u32[]{:S(2)}) copy-start(f32[2,8192]{1,0:T(2,128)} %param.12) | copy-start | bytes 196612
  168.4 221.3 %all-gather.3.cloned.1.call-start = ((), (), s32[]{:S(2)}) async-start(), calls=%async_computation.1 | async-start | bytes 1081344 | tf_op jit(solution)/shard_map/all_gather | solution.py:49
Sparse Core Ops, SparseCore 0:
  168.5 124.1 all-reduce.3
  297.2 92.4 all-gather.2
where the time goes:
time: 399 us
  waiting for transfers between devices  191 us (48%)
  blocking collectives  185 us (46%)
  between operations  15.5 us (4%)
    unnamed x1, blocking collectives  157 us
    psum x1, waiting for transfers between devices, on_device(): total_rows, total_count = lax.psum((weighted, weight), 'group')  95.9 us
    all_gather x1, waiting for transfers between devices, on_device(): lax.all_gather(master_new.astype(jnp.bfloat16), 'fsdp', axis=0, tiled=True)  94.7 us
    psum x1, blocking collectives, on_device(): total_rows, total_count = lax.psum((weighted, weight), 'group')  28.3 us
  transfers between devices with their start and end apart: 2, of which 2 were waited for; matrix products, arithmetic and copies ran while one was open for 0% of the time, Pallas kernels for 0%

commit v1 on v0

v1 whole, which is shorter than its diff:
```python
import jax
import jax.numpy as jnp
from jax import lax
from jax.experimental import pallas as pl
from jax.experimental.pallas import tpu as pltpu
from jax.sharding import PartitionSpec as P

BLOCK = 256
STEP = 500
MESH = pl.DeviceIdType.MESH
F32 = jnp.float32
CODE = 27408.0


def far_first(i):
    j = i // 2
    off = jnp.where(j % 2 == 1, 8 - (j + 1) // 2, j // 2)
    return (4 + off) % 8, 1 - i % 2


def place():
    g = lax.axis_index("group")
    f = lax.axis_index("fsdp")
    return g // 2, g % 2, f // 16, (f // 2) % 8, f % 2


def fsdp_peer(i, sign, xh, z, core):
    dz, dx = far_first(i)
    return (xh + dx) % 2, (z + 8 + sign * dz) % 8


def group_peer(i, sign, y, xl):
    dy, dx = far_first(i)
    return ((y + 8 + sign * dy) % 8) * 2 + (xl + dx) % 2


def kernel(
    grad, master, drift, mom, mcode, scode, mscale, sscale, counts,
    o_master, o_mom, o_m, o_s, o_model,
    loc, sib, out_code, in_code, old_m, old_s, weighted, part, mean, w_out, w_in,
    new_master, new_mom, new_m, new_s, copy16, in16,
    s_loc, s_sib, r_sib, s_code, r_code, s_w, r_w, s_part, r_part, s_mean, r_mean, s_mod, r_mod,
    s_fwd, r_fwd, s_own, s_out,
):
    y, xl, xh, z, core = place()
    me_g = y * 2 + xl
    me_f = xh * 16 + z * 2 + core
    sibling = (me_g, me_f + 1 - 2 * core)

    def chip(i, sign=1):
        px, pz = fsdp_peer(i, sign, xh, z, core)
        return px * 4 + pz // 2, pz % 2, (me_g, px * 16 + pz * 2 + core)

    def peer(i):
        return (group_peer(i, 1, y, xl), me_f)

    barrier = pltpu.get_barrier_semaphore()
    pl.semaphore_signal(barrier, inc=1, device_id=sibling, device_id_type=MESH)

    def greet(i, _):
        pl.semaphore_signal(barrier, inc=1, device_id=chip(i)[2], device_id_type=MESH)
        pl.semaphore_signal(barrier, inc=1, device_id=peer(i), device_id_type=MESH)
        return 0

    lax.fori_loop(0, 15, greet, 0)

    def local_copy(i):
        t, par, _ = chip(i)
        return pltpu.make_async_copy(grad.at[t, :, par * 2 + core], loc.at[i], s_loc.at[i])

    def sibling_copy(i):
        t, par, _ = chip(i)
        return pltpu.make_async_remote_copy(
            grad.at[t, :, par * 2 + 1 - core], sib.at[i], s_sib.at[i], r_sib.at[i],
            device_id=sibling, device_id_type=MESH,
        )

    def code_copy(i):
        return pltpu.make_async_remote_copy(
            out_code.at[i], in_code.at[i], s_code.at[i], r_code.at[i],
            device_id=chip(i)[2], device_id_type=MESH,
        )

    def w_copy(i):
        return pltpu.make_async_remote_copy(
            w_out, w_in.at[i], s_w.at[i], r_w.at[i], device_id=peer(i), device_id_type=MESH
        )

    def part_copy(i):
        to = group_peer(i, 1, y, xl)
        return pltpu.make_async_remote_copy(
            weighted.at[pl.ds(pl.multiple_of(to * 8, 8), 8)], part.at[i], s_part.at[i], r_part.at[i],
            device_id=(to, me_f), device_id_type=MESH,
        )

    mine = pl.ds(pl.multiple_of(me_g * 8, 8), 8)

    def mean_copy(i, source):
        at = pl.ds(pl.multiple_of(source * 8, 8), 8)
        return pltpu.make_async_remote_copy(
            mean.at[at], mean.at[at], s_mean.at[i], r_mean.at[i], device_id=peer(i), device_id_type=MESH
        )

    def model_copy(i):
        return pltpu.make_async_remote_copy(
            copy16, in16.at[i], s_mod.at[i], r_mod.at[i], device_id=chip(i)[2], device_id_type=MESH
        )

    def row_at(i):
        t, par, _ = chip(i, -1)
        return t, par * 2

    def own_store(i, source):
        t, s = row_at(i)
        return pltpu.make_async_copy(source, o_model.at[t, :, s + core], s_own.at[i])

    def forward(i, source, whose):
        t, s = row_at(i)
        return pltpu.make_async_remote_copy(
            source, o_model.at[t, :, s + whose], s_fwd.at[i], r_fwd.at[i],
            device_id=sibling, device_id_type=MESH,
        )

    def each(n, f):
        def body(i, _):
            f(i)
            return 0

        lax.fori_loop(0, n, body, 0)

    each(16, lambda i: local_copy(i).start())
    weight = counts[0].astype(F32)
    w_out[...] = jnp.full((8, 128), weight, F32)

    rows = lax.broadcasted_iota(jnp.int32, (128, 32), 0)
    hit = lax.broadcasted_iota(jnp.int32, (128, 32), 1) == rows // 4

    def scale_of(ref):
        both = jnp.where(rows % 2 == 0, ref[0, 0:1, :], ref[0, 1:2, :])
        return jnp.sum(jnp.where(hit, both, 0.0), axis=1, keepdims=True)

    signed = (mcode[...].astype(F32) - 127.5) / 127.5
    old_m[...] = 0.9 * (signed * signed * signed * scale_of(mscale))
    unsigned = (scode[...].astype(F32) + 16.0) / 271.0
    old_s[...] = 0.999 * (unsigned * unsigned * scale_of(sscale))

    pl.semaphore_wait(barrier, 31)
    each(16, lambda i: sibling_copy(i).start())
    each(15, lambda i: w_copy(i).start())

    def pair(i):
        local_copy(i).wait()
        sibling_copy(i).wait_recv()
        return (
            loc.at[i].reshape(128, 128)[...].astype(F32) + sib.at[i].reshape(128, 128)[...].astype(F32)
        )

    def encode(i):
        out_code[i] = jnp.round(pair(i) * CODE).astype(jnp.int32).astype(jnp.int16)
        code_copy(i).start()

    each(15, encode)
    own = pair(15)

    def decode(i, total):
        code_copy(i).wait_recv()
        return total + in_code[i].astype(jnp.int32)

    total = lax.fori_loop(0, 15, decode, jnp.zeros((128, 128), jnp.int32))
    g = own + total.astype(F32) * (1.0 / CODE)
    moment = old_m[...] + 0.1 * g
    second = old_s[...] + 0.001 * g * g
    new_m[...] = moment
    new_s[...] = second
    update = moment / (1.0 - 0.9**STEP) / (jnp.sqrt(second / (1.0 - 0.999**STEP)) + 1e-08)
    inner = master[...] + drift[...]
    pseudo = master[...] - (inner - 0.8 * (update + 0.025 * inner))
    weighted[...] = weight * pseudo

    each(15, lambda i: part_copy(i).start())
    out_m = pltpu.make_async_copy(new_m, o_m, s_out.at[0])
    out_s = pltpu.make_async_copy(new_s, o_s, s_out.at[1])
    out_m.start()
    out_s.start()

    def add_weight(i, total):
        w_copy(i).wait_recv()
        return total + w_in[i]

    all_weights = lax.fori_loop(0, 15, add_weight, w_out[...])

    def add_part(i, total):
        part_copy(i).wait_recv()
        return total + part[i]

    mean[mine, :] = lax.fori_loop(0, 15, add_part, weighted[mine, :]) / all_weights
    each(15, lambda i: mean_copy(i, me_g).start())
    each(15, lambda i: mean_copy(i, group_peer(i, -1, y, xl)).wait_recv())

    momentum = 0.9 * mom[...] + mean[...]
    fresh = master[...] - 0.7 * (mean[...] + 0.9 * momentum)
    copy16.reshape(128, 128)[...] = fresh.astype(jnp.bfloat16)
    each(15, lambda i: model_copy(i).start())
    own_store(15, copy16).start()
    forward(15, copy16, core).start()
    new_mom[...] = momentum
    new_master[...] = fresh
    out_mom = pltpu.make_async_copy(new_mom, o_mom, s_out.at[2])
    out_master = pltpu.make_async_copy(new_master, o_master, s_out.at[3])
    out_mom.start()
    out_master.start()

    def pass_on(i):
        model_copy(i).wait_recv()
        forward(i, in16.at[i], core).start()
        own_store(i, in16.at[i]).start()

    each(15, pass_on)

    def finish(i):
        sibling_copy(i).wait_send()
        forward(i, copy16, core).wait_send()
        forward(i, copy16, 1 - core).wait_recv()
        own_store(i, copy16).wait()

    each(16, finish)

    def finish_sends(i):
        code_copy(i).wait_send()
        w_copy(i).wait_send()
        part_copy(i).wait_send()
        mean_copy(i, me_g).wait_send()
        model_copy(i).wait_send()

    each(15, finish_sends)
    out_m.wait()
    out_s.wait()
    out_mom.wait()
    out_master.wait()


def outer_step(*args):
    any_space = pl.BlockSpec(memory_space=pl.ANY)
    vmem = pl.BlockSpec(memory_space=pltpu.VMEM)
    flat = jax.ShapeDtypeStruct((128, 128), F32)
    dma = pltpu.SemaphoreType.DMA
    rows16 = lambda n: pltpu.VMEM((n, 64, 2, 128), jnp.bfloat16)
    square = pltpu.VMEM((128, 128), F32)
    return pl.pallas_call(
        kernel,
        out_shape=(flat, flat, flat, flat, jax.ShapeDtypeStruct((8, 64, 4, 2, 128), jnp.bfloat16)),
        in_specs=[any_space] + [vmem] * 7 + [pl.BlockSpec(memory_space=pltpu.SMEM)],
        out_specs=(any_space,) * 5,
        scratch_shapes=[
            rows16(16), rows16(16),
            pltpu.VMEM((15, 128, 128), jnp.int16), pltpu.VMEM((15, 128, 128), jnp.int16),
            square, square, square, pltpu.VMEM((15, 8, 128), F32), square,
            pltpu.VMEM((8, 128), F32), pltpu.VMEM((15, 8, 128), F32),
            square, square, square, square,
            pltpu.VMEM((64, 2, 128), jnp.bfloat16), rows16(15),
            dma((16,)), dma((16,)), dma((16,)), dma((15,)), dma((15,)), dma((15,)), dma((15,)),
            dma((15,)), dma((15,)), dma((15,)), dma((15,)), dma((15,)), dma((15,)),
            dma((16,)), dma((16,)), dma((16,)), dma((4,)),
        ],
        compiler_params=pltpu.CompilerParams(
            collective_id=0, has_side_effects=True, vmem_limit_bytes=16 * 1024 * 1024
        ),
        name="outer_step",
    )(*args)


def hand_over(*refs):
    sems = refs[-1]
    copies = [pltpu.make_async_copy(refs[k], refs[5 + k], sems.at[k]) for k in (4, 0, 1, 2, 3)]
    for c in copies:
        c.start()
    for c in copies:
        c.wait()


def on_device(grad_terms, master, inner_drift, momentum, moment_codes, second_codes, moment_scale, second_scale, counts):
    def to_flat(x):
        return x.reshape(2, 64, 128).transpose(1, 0, 2).reshape(128, 128)

    def from_flat(x):
        return x.reshape(64, 2, 128).transpose(1, 0, 2).reshape(2, 8192)

    grad = grad_terms.reshape(8, 4, 2, 64, 128).transpose(0, 3, 1, 2, 4)
    outs = outer_step(
        grad, to_flat(master), to_flat(inner_drift), to_flat(momentum),
        to_flat(moment_codes), to_flat(second_codes), moment_scale, second_scale, counts,
    )
    any_space = pl.BlockSpec(memory_space=pl.ANY)
    a, b, c, d, e = pl.pallas_call(
        hand_over,
        out_shape=tuple(jax.ShapeDtypeStruct(o.shape, o.dtype) for o in outs),
        in_specs=[any_space] * 5,
        out_specs=(any_space,) * 5,
        scratch_shapes=[pltpu.SemaphoreType.DMA((5,))],
        name="hand_over",
    )(*outs)
    return (
        from_flat(a), from_flat(b), from_flat(c)[None], from_flat(d)[None],
        e.transpose(0, 2, 3, 1, 4).reshape(64, 8192),
    )


def solution(mesh):
    rows = P("fsdp", None)
    both = P("group", "fsdp", None)
    return jax.shard_map(
        on_device,
        mesh=mesh,
        in_specs=(P("group", "fsdp", None, None), rows, both, rows, both, both, both, both, P("group")),
        out_specs=(rows, rows, both, both, P()),
        check_vma=False,
    )
```

time: 399 us -> 111 us (0.28)
  waiting for transfers between devices: 191 us -> 0 us
  blocking collectives: 185 us -> 0 us
  Pallas kernels: 0 us -> 99.3 us
  between operations: 15.5 us -> 1.32 us
  local copies, waits for them, and re-layouts: 3.77 us -> 9.57 us
    unnamed x1 -> x0, blocking collectives: 157 us -> none
    pallas_call x0 -> x2, Pallas kernels: none -> 99.3 us  [the longest x1 58.4 us: outer_step(): pl.pallas_call(kernel, out_shape=(flat, flat, flat, flat, jax.ShapeDtypeS...]
    psum x1 -> x0, waiting for transfers between devices: 95.9 us -> none  [on_device(): total_rows, total_count = lax.psum((weighted, weight), 'group')]
    all_gather x1 -> x0, waiting for transfers between devices: 94.7 us -> none  [on_device(): lax.all_gather(master_new.astype(jnp.bfloat16), 'fsdp', axis=0, tiled=True)]
    psum x1 -> x0, blocking collectives: 28.3 us -> none  [on_device(): total_rows, total_count = lax.psum((weighted, weight), 'group')]
    unnamed x16 -> x26, local copies, waits for them, and re-layouts: 3.54 us -> 9.57 us
  transfers between devices with their start and end apart: 2 -> 0, of which waited for: 2 -> 0; matrix products, arithmetic and copies ran while one was open for 0% -> 0% of each run, Pallas kernels for 0% -> 0%
where the time goes in v1:
time: 111 us; the launch traced here: 110 us
  Pallas kernels  99.3 us (89%)
  local copies, waits for them, and re-layouts  9.57 us (9%)
  between operations  1.32 us (1%)
    pallas_call x1, Pallas kernels, outer_step(): pl.pallas_call(kernel, out_shape=(flat, flat, flat, flat, jax.ShapeDtypeS...  58.4 us
    pallas_call x1, Pallas kernels, on_device(): pl.pallas_call(hand_over, out_shape=tuple((jax.ShapeDtypeStruct(o.shape,...  40.8 us
    unnamed x26, local copies, waits for them, and re-layouts  9.57 us

profile of v1, /device:TPU:1, one launch (start us, length us, event | category | flops | bytes accessed | tf_op | source)
XLA Modules:
  0.0 110.2 jit_solution(3882138320232089453)
XLA Ops:
  1.3 0.0 copy-start.12
  1.3 0.0 copy-start.11
  1.3 0.7 copy-done.12
  2.0 0.0 copy-done.11
  2.0 0.0 copy-start.1
  2.0 1.2 %copy-done.1 = bf16[1,1,64,8192]{3,2,1,0:T(8,128)(2,1)S(1)} copy-done((bf16[1,1,64,8192]{3,2,1,0:T(8,128)(2,1)S(1)}, bf16[1,1,64,8192]{3,2,1,0:T(8,128)(2,1)}, u32[]{:S(2)}) %copy-start.1) | copy-done | bytes 1048600
  3.2 0.0 copy-start.2
  3.2 0.8 copy-done.2
  4.0 0.0 copy-start.3
  4.0 0.8 copy-done.3
  4.9 0.0 copy-start.4
  4.9 0.8 copy-done.4
  5.7 0.0 copy-start.5
  5.7 0.8 copy-done.5
  6.6 0.0 copy-start.6
  6.6 0.8 copy-done.6
  7.4 58.4 %outer_step.1 = (f32[128,128]{1,0:T(8,128)S(1)}, f32[128,128]{1,0:T(8,128)S(1)}, f32[128,128]{1,0:T(8,128)S(1)}, f32[128,128]{1,0:T(8,128)S(1)}, bf16[8,64,4,2,128]{4,3,2,1,0:T(2,128)(2,1)S(1)}) custom-call(bf16[8,64,4,2,128]{4,3,2,1,0:T(2,128)(2,1)S(1)} %bitcast.51, f32[128,128]{1,0:T(8,128)S(1)} %bitcast.52, f32[128,128]{1,0:T(8,128)S(1)} %bitcast.53, ...), custom_call_target="tpu_custom_call" | custom-call | tf_op jit(solution)/shard_map/outer_step/pallas_call | solution.py:249
  65.8 0.0 copy-start
  65.8 1.0 copy-done
  66.8 0.0 copy-start.7
  66.8 0.6 copy-done.7
  67.4 0.0 copy-start.8
  67.4 0.6 copy-done.8
  68.0 0.0 copy-start.9
  68.0 0.6 copy-done.9
  68.7 0.0 copy-start.10
  68.7 0.6 copy-done.10
  69.3 40.8 %hand_over.1 = (f32[128,128]{1,0:T(8,128)}, f32[128,128]{1,0:T(8,128)}, f32[128,128]{1,0:T(8,128)}, f32[128,128]{1,0:T(8,128)}, bf16[8,64,4,2,128]{4,3,2,1,0:T(2,128)(2,1)}) custom-call(f32[128,128]{1,0:T(8,128)} %copy-done.7, f32[128,128]{1,0:T(8,128)} %copy-done.8, f32[128,128]{1,0:T(8,128)} %copy-done.9, f32[128,128]{1,0:T(8,128)} %copy-done.10, ...), custom_call_target="tpu_custom_call" | custom-call | tf_op jit(solution)/shard_map/hand_over/pallas_call | solution.py:294
Async XLA Ops:
  1.3 0.7 copy-start.12
  1.3 0.7 copy-start.11
  2.0 1.2 %copy-start.1 = (bf16[1,1,64,8192]{3,2,1,0:T(8,128)(2,1)S(1)}, bf16[1,1,64,8192]{3,2,1,0:T(8,128)(2,1)}, u32[]{:S(2)}) copy-start(bf16[1,1,64,8192]{3,2,1,0:T(8,128)(2,1)} %param.9) | copy-start | bytes 3145732
  3.2 0.8 copy-start.2
  4.0 0.8 copy-start.3
  4.9 0.8 copy-start.4
  5.7 0.8 copy-start.5
  6.6 0.8 copy-start.6
  65.8 1.0 copy-start
  66.8 0.6 copy-start.7
  67.4 0.6 copy-start.8
  68.0 0.6 copy-start.9
  68.7 0.6 copy-start.10

commit v2 on v0

v2 whole, which is shorter than its diff:
```python
import jax
import jax.numpy as jnp
from jax import lax
from jax.experimental import pallas as pl
from jax.experimental.pallas import tpu as pltpu
from jax.sharding import PartitionSpec as P

BLOCK = 256
STEP = 500
MESH = pl.DeviceIdType.MESH
F32 = jnp.float32
BF16 = jnp.bfloat16
CODE = 27408.0
RING = (4, 3, 5, 2, 6, 1, 7, 0)
PEERS = tuple((dy, dx) for dy in RING for dx in (1, 0))[:15]


def kernel(
    grad, master_in, drift_in, mom_in, mcode_in, scode_in, mscale_in, sscale_in, counts,
    o_master, o_mom, o_m, o_s, o_model,
    terms, sib, master, drift, mom, mcode, scode, mscale, sscale,
    pairs, out_code, in_code, summed, old_m, old_s, weighted, part, mean, w_out, w_in, order, slice_out, slice_in,
    s_in, s_sib, r_sib, s_code, r_code, s_w, r_w, s_part, r_part, s_mean, r_mean, s_slice, r_slice, s_block, r_block,
    s_fwd, r_fwd,
):
    g = lax.axis_index("group")
    f = lax.axis_index("fsdp")
    y, xl = g // 2, g % 2
    xh, z, core = f // 16, (f // 2) % 8, f % 2
    other = 1 - core
    across = (xh + core) % 2
    zs = [lax.rem(z + d, 8) for d in range(8)]
    ys = [lax.rem(y + d, 8) * 2 for d in range(8)]
    back_ys = [lax.rem(y + 8 - d, 8) * 2 for d in range(8)]
    xls = [xl, 1 - xl]

    def at(px, pz, pc):
        return (g, px * 16 + pz * 2 + pc)

    sibling = at(xh, z, other)

    def remote(source, target, send, recv, device):
        return pltpu.make_async_remote_copy(
            source, target, send, recv, device_id=device, device_id_type=MESH
        )

    loads = [
        pltpu.make_async_copy(grad.at[pl.ds(16 * k, 16)], terms.at[pl.ds(16 * k, 16)], s_in.at[k])
        for k in range(4)
    ]
    small = [
        pltpu.make_async_copy(a, b, s_in.at[4 + k])
        for k, (a, b) in enumerate((
            (mscale_in, mscale), (sscale_in, sscale), (mcode_in, mcode), (scode_in, scode),
            (master_in, master), (drift_in, drift), (mom_in, mom),
        ))
    ]
    for c in loads + small:
        c.start()

    barrier = pltpu.get_barrier_semaphore()

    def greet(device):
        pl.semaphore_signal(barrier, inc=1, device_id=device, device_id_type=MESH)

    for d in RING:
        greet(at(1 - core, zs[d], xh))
        greet(at(core, zs[d], 1 - core))
        if d:
            greet(at(core, zs[d], core))
    pl.when(across == 1)(lambda: greet(at(core, z, core)))
    for dy, dx in PEERS:
        greet((ys[dy] + xls[dx], f))

    for c in small[:4]:
        c.wait()
    weight = counts[0].astype(F32)
    w_out[...] = jnp.full((8, 128), weight, F32)
    rows = lax.broadcasted_iota(jnp.int32, (128, 32), 0)
    hit = lax.broadcasted_iota(jnp.int32, (128, 32), 1) == rows // 4

    def scale_of(ref):
        both = jnp.where(rows % 2 == 0, ref[0, 0:1, :], ref[0, 1:2, :])
        return jnp.sum(jnp.where(hit, both, 0.0), axis=1, keepdims=True)

    signed = (mcode[...].astype(F32) - 127.5) / 127.5
    old_m[...] = 0.9 * (signed * signed * signed * scale_of(mscale))
    unsigned = (scode[...].astype(F32) + 16.0) / 271.0
    old_s[...] = 0.999 * (unsigned * unsigned * scale_of(sscale))
    for c in loads:
        c.wait()

    pl.semaphore_wait(barrier, 38 + across)

    halves = [1 - z // 4, z // 4]

    def half_rows(owner, k):
        return pl.ds(pl.multiple_of(owner * 32 + halves[k] * 16, 16), 16)

    swaps = [
        remote(terms.at[half_rows(other, k)], sib.at[k], s_sib.at[k], r_sib.at[k], sibling) for k in range(2)
    ]
    for c in swaps:
        c.start()

    group_at = [ys[dy] + xls[dx] for dy, dx in PEERS]
    group_from = [back_ys[dy] + xls[dx] for dy, dx in PEERS]
    w_copies = [remote(w_out, w_in.at[i], s_w.at[i], r_w.at[i], (p, f)) for i, p in enumerate(group_at)]
    for c in w_copies:
        c.start()

    for k in range(2):
        swaps[k].wait_recv()

        def add_pair(j, _, k=k):
            columns = pl.ds(pl.multiple_of(j * 128, 128), 128)
            both = terms[half_rows(core, k), columns].astype(F32) + sib[k, :, columns].astype(F32)
            pairs[pl.ds(pl.multiple_of(j * 16, 16), 16), :] = both * CODE
            return 0

        lax.fori_loop(0, 64, add_pair, 0, unroll=4)
        for q in range(4):
            pz = halves[k] * 4 + q
            ahead = lax.rem(pz - z + 8, 8)
            slot = across * 8 + ahead
            for pc in range(2):
                n = k * 8 + q * 2 + pc
                for big in range(8):
                    two = [pairs[pl.ds(big * 128 + q * 4 + pc * 2 + r, 8, stride=16), :] for r in range(2)]
                    whole = jnp.round(jnp.concatenate(two, axis=0)).astype(jnp.int32)
                    out_code[n, big * 16 : big * 16 + 16, :] = whole.astype(jnp.int16)
                copy = remote(
                    out_code.at[n], in_code.at[slot], s_code.at[n], r_code.at[slot], at(core, pz, pc)
                )
                if k == 0:
                    copy.start()
                else:
                    stays = (ahead == 0) & (across == 0) & (core == pc)
                    pl.when(jnp.logical_not(stays))(copy.start)

                    @pl.when(stays)
                    def _(n=n):
                        in_code[0] = out_code[n]

    def code_wait(slot):
        remote(out_code.at[0], in_code.at[slot], s_code.at[0], r_code.at[slot], sibling).wait_recv()

    total = jnp.zeros((128, 128), jnp.int32)
    for d in RING:
        for dx in range(2):
            slot = dx * 8 + d
            if slot:
                code_wait(slot)
            else:
                pl.when(xh != core)(lambda: code_wait(0))
            total = total + in_code[slot].astype(jnp.int32)
    total = total.astype(F32) * (1.0 / CODE)
    for big in range(8):
        for r in range(2):
            summed[pl.ds(big * 16 + r, 8, stride=2), :] = total[big * 16 + r * 8 : big * 16 + r * 8 + 8]

    for c in small[4:]:
        c.wait()
    grad_sum = summed[...]
    moment = old_m[...] + 0.1 * grad_sum
    second = old_s[...] + 0.001 * grad_sum * grad_sum
    update = moment / (1.0 - 0.9**STEP) / (jnp.sqrt(second / (1.0 - 0.999**STEP)) + 1e-08)
    inner = master[...] + drift[...]
    pseudo = master[...] - (inner - 0.8 * (update + 0.025 * inner))
    weighted[...] = weight * pseudo

    def eight(p):
        return pl.ds(pl.multiple_of(p * 8, 8), 8)

    part_copies = [
        remote(weighted.at[eight(p)], part.at[i], s_part.at[i], r_part.at[i], (p, f))
        for i, p in enumerate(group_at)
    ]
    for c in part_copies:
        c.start()
    o_m[...] = moment
    o_s[...] = second
    all_weights = w_out[...]
    for i in range(15):
        w_copies[i].wait_recv()
        all_weights = all_weights + w_in[i]
    own_sum = weighted[eight(g), :]
    for i in range(15):
        part_copies[i].wait_recv()
        own_sum = own_sum + part[i]
    own_mean = own_sum / all_weights

    def nesterov(at_rows, mean_pseudo):
        momentum = 0.9 * mom[at_rows, :] + mean_pseudo
        return master[at_rows, :] - 0.7 * (mean_pseudo + 0.9 * momentum), momentum

    fresh, _ = nesterov(eight(g), own_mean)
    order[...] = fresh
    slice_out[0:4, :] = order[pl.ds(0, 4, stride=2), :]
    slice_out[4:8, :] = order[pl.ds(1, 4, stride=2), :]
    mean[eight(g), :] = own_mean
    slice_copies = []
    for d in RING:
        for dx in (1, 0):
            slot = ((8 - d) % 8) * 2
            to = at((xh + dx) % 2, zs[d], xh)
            n = d * 2 + dx
            where = z * 2 + core
            copy = remote(slice_out, slice_in.at[where], s_slice.at[n], r_slice.at[where], to)
            slice_copies.append(copy)
            if d or dx:
                copy.start()
            else:
                pl.when(xh != core)(copy.start)

                @pl.when(xh == core)
                def _():
                    slice_in[where] = slice_out[...]

    mean_copies = []
    for i, p in enumerate(group_at):
        c = remote(mean.at[eight(g)], mean.at[eight(g)], s_mean.at[i], r_mean.at[i], (p, f))
        c.start()
        mean_copies.append(c)

    def slice_wait(where):
        remote(slice_out, slice_in.at[where], s_slice.at[0], r_slice.at[where], sibling).wait_recv()

    for k in range(8):
        for pc in range(2):
            stays = (xh == core) & (z == k) & (core == pc)
            pl.when(jnp.logical_not(stays))(lambda w=k * 2 + pc: slice_wait(w))
    mine = pl.ds(pl.multiple_of(core * 32, 32), 32)
    flat = slice_in.reshape(128, 128)

    def columns_of(p):
        return pl.ds(pl.multiple_of(p * 512, 512), 512)

    for k in range(2):
        for j in range(4):
            two = [flat[pl.ds((k * 16 + h * 8) * 4 + j, 8, stride=4), :] for h in range(2)]
            o_model[
                pl.ds(pl.multiple_of(core * 32 + k * 16, 16), 16),
                pl.ds(pl.multiple_of(g * 512 + j * 128, 128), 128),
            ] = jnp.concatenate(two, axis=0).astype(BF16)

    def block(p):
        return o_model.at[mine, columns_of(p)]

    block_copies = [
        remote(block(g), block(g), s_block.at[i], r_block.at[i], (p, f)) for i, p in enumerate(group_at)
    ]
    for c in block_copies:
        c.start()
    fwd = [remote(block(g), block(g), s_fwd.at[15], r_fwd.at[15], sibling)]
    fwd[0].start()

    for i, p in enumerate(group_from):
        remote(mean.at[eight(p)], mean.at[eight(p)], s_mean.at[i], r_mean.at[i], sibling).wait_recv()
    everything = pl.ds(0, 128)
    o_master[...], o_mom[...] = nesterov(everything, mean[...])

    for i, p in enumerate(group_from):
        remote(block(p), block(p), s_block.at[i], r_block.at[i], sibling).wait_recv()
        c = remote(block(p), block(p), s_fwd.at[i], r_fwd.at[i], sibling)
        c.start()
        fwd.append(c)

    theirs = pl.ds(pl.multiple_of(other * 32, 32), 32)
    for i, p in enumerate(group_from + [g]):
        there = o_model.at[theirs, columns_of(p)]
        remote(there, there, s_fwd.at[i], r_fwd.at[i], sibling).wait_recv()

    for c in swaps + w_copies + part_copies + mean_copies + block_copies + fwd + slice_copies[:15]:
        c.wait_send()
    pl.when(xh != core)(slice_copies[15].wait_send)
    for n in range(16):
        k, q, pc = n // 8, n // 2 % 4, n % 2
        ahead = lax.rem(halves[k] * 4 + q - z + 8, 8)
        done = remote(out_code.at[n], in_code.at[0], s_code.at[n], r_code.at[0], sibling)
        stays = (ahead == 0) & (across == 0) & (core == pc)
        if k == 0:
            done.wait_send()
        else:
            pl.when(jnp.logical_not(stays))(done.wait_send)


def outer_step(*args):
    hbm = pl.BlockSpec(memory_space=pltpu.HBM)
    vmem = pl.BlockSpec(memory_space=pltpu.VMEM)
    square = pltpu.VMEM((128, 128), F32)
    codes = pltpu.VMEM((128, 128), jnp.int32)
    eight = lambda n: pltpu.VMEM((n, 8, 128), F32)
    dma = pltpu.SemaphoreType.DMA
    out = pltpu.VMEM((128, 128), F32)
    return pl.pallas_call(
        kernel,
        out_shape=(out, out, out, out, pltpu.VMEM((64, 8192), BF16)),
        in_specs=[hbm] * 8 + [pl.BlockSpec(memory_space=pltpu.SMEM)],
        out_specs=(vmem,) * 5,
        scratch_shapes=[
            pltpu.VMEM((64, 8192), BF16), pltpu.VMEM((2, 16, 8192), BF16),
            square, square, square, codes, codes, pltpu.VMEM((1, 2, 32), F32), pltpu.VMEM((1, 2, 32), F32),
            pltpu.VMEM((1024, 128), F32), pltpu.VMEM((16, 128, 128), jnp.int16), pltpu.VMEM((16, 128, 128), jnp.int16),
            square, square, square, square, eight(15), square,
            pltpu.VMEM((8, 128), F32), eight(15), pltpu.VMEM((8, 128), F32), pltpu.VMEM((8, 128), F32), eight(16),
            dma((11,)), dma((2,)), dma((2,)), dma((16,)), dma((16,)), dma((15,)), dma((15,)), dma((15,)), dma((15,)),
            dma((15,)), dma((15,)), dma((16,)), dma((16,)), dma((15,)), dma((15,)), dma((16,)), dma((16,)),
        ],
        compiler_params=pltpu.CompilerParams(
            collective_id=0, has_side_effects=True, vmem_limit_bytes=16 * 1024 * 1024
        ),
        name="outer_step",
    )(*args)


def hand_over(*refs):
    sems = refs[-1]
    copies = [pltpu.make_async_copy(refs[k], refs[5 + k], sems.at[k]) for k in (4, 0, 1, 2, 3)]
    for c in copies:
        c.start()
    for c in copies:
        c.wait()


def on_device(grad_terms, master, inner_drift, momentum, moment_codes, second_codes, moment_scale, second_scale, counts):
    def to_flat(x):
        return x.reshape(2, 64, 128).transpose(1, 0, 2).reshape(128, 128)

    def from_flat(x):
        return x.reshape(64, 2, 128).transpose(1, 0, 2).reshape(2, 8192)

    operands = (
        grad_terms[0, 0], to_flat(master), to_flat(inner_drift), to_flat(momentum),
        to_flat(moment_codes), to_flat(second_codes), moment_scale, second_scale,
    )
    outs = outer_step(*(pltpu.with_memory_space_constraint(x, pltpu.HBM) for x in operands), counts)
    a, b, c, d, model = pl.pallas_call(
        hand_over,
        out_shape=tuple(jax.ShapeDtypeStruct(o.shape, o.dtype) for o in outs),
        in_specs=[pl.BlockSpec(memory_space=pltpu.VMEM)] * 5,
        out_specs=(pl.BlockSpec(memory_space=pltpu.HBM),) * 5,
        scratch_shapes=[pltpu.SemaphoreType.DMA((5,))],
        name="hand_over",
    )(*(pltpu.with_memory_space_constraint(o, pltpu.VMEM) for o in outs))
    return from_flat(a), from_flat(b), from_flat(c)[None], from_flat(d)[None], model


def solution(mesh):
    rows = P("fsdp", None)
    both = P("group", "fsdp", None)
    return jax.shard_map(
        on_device,
        mesh=mesh,
        in_specs=(P("group", "fsdp", None, None), rows, both, rows, both, both, both, both, P("group")),
        out_specs=(rows, rows, both, both, P()),
        check_vma=False,
    )
```

time: 399 us -> 62.2 us (0.16)
  waiting for transfers between devices: 191 us -> 0 us
  blocking collectives: 185 us -> 0 us
  Pallas kernels: 0 us -> 60.7 us
  between operations: 15.5 us -> 1.29 us
    unnamed x1 -> x0, blocking collectives: 157 us -> none
    psum x1 -> x0, waiting for transfers between devices: 95.9 us -> none  [on_device(): total_rows, total_count = lax.psum((weighted, weight), 'group')]
    all_gather x1 -> x0, waiting for transfers between devices: 94.7 us -> none  [on_device(): lax.all_gather(master_new.astype(jnp.bfloat16), 'fsdp', axis=0, tiled=True)]
    pallas_call x0 -> x2, Pallas kernels: none -> 60.7 us  [the longest x1 59.6 us: outer_step(): pl.pallas_call(kernel, out_shape=(out, out, out, out, pltpu.VMEM((64, 819...]
    psum x1 -> x0, blocking collectives: 28.3 us -> none  [on_device(): total_rows, total_count = lax.psum((weighted, weight), 'group')]
  transfers between devices with their start and end apart: 2 -> 0, of which waited for: 2 -> 0; matrix products, arithmetic and copies ran while one was open for 0% -> 0% of each run, Pallas kernels for 0% -> 0%
where the time goes in v2:
time: 62.2 us; the launch traced here: 62 us
  Pallas kernels  60.7 us (98%)
  between operations  1.29 us (2%)
    pallas_call x1, Pallas kernels, outer_step(): pl.pallas_call(kernel, out_shape=(out, out, out, out, pltpu.VMEM((64, 819...  59.6 us

profile of v2, /device:TPU:1, one launch (start us, length us, event | category | flops | bytes accessed | tf_op | source)
XLA Modules:
  0.0 62.0 jit_solution(17539425012894314794)
XLA Ops:
  1.3 59.6 %outer_step.1 = (f32[128,128]{1,0:T(8,128)S(1)}, f32[128,128]{1,0:T(8,128)S(1)}, f32[128,128]{1,0:T(8,128)S(1)}, f32[128,128]{1,0:T(8,128)S(1)}, bf16[64,8192]{1,0:T(8,128)(2,1)S(1)}) custom-call(bf16[64,8192]{1,0:T(8,128)(2,1)} %bitcast.46, f32[128,128]{1,0:T(8,128)} %bitcast.47, f32[128,128]{1,0:T(8,128)} %bitcast.48, f32[128,128]{1,0:T(8,128)} %bitcast.49, ...), custom_call_target="tpu_custom_call" | custom-call | tf_op jit(solution)/shard_map/outer_step/pallas_call | solution.py:296
  60.9 1.1 %hand_over.1 = (f32[128,128]{1,0:T(8,128)}, f32[128,128]{1,0:T(8,128)}, f32[128,128]{1,0:T(8,128)}, f32[128,128]{1,0:T(8,128)}, bf16[64,8192]{1,0:T(8,128)(2,1)}) custom-call(f32[128,128]{1,0:T(8,128)S(1)} %get-tuple-element.15.refs_0_, f32[128,128]{1,0:T(8,128)S(1)} %get-tuple-element.16.refs_1_, f32[128,128]{1,0:T(8,128)S(1)} %get-tuple-element.17.refs_2_, ...), custom_call_target="tpu_custom_call" | custom-call | tf_op jit(solution)/shard_map/hand_over/pallas_call | solution.py:338

commit v3 on v2

--- a/solution.py
+++ b/solution.py
@@ -13,6 +13,8 @@
 CODE = 27408.0
 RING = (4, 3, 5, 2, 6, 1, 7, 0)
 PEERS = tuple((dy, dx) for dy in RING for dx in (1, 0))[:15]
+PLANE = tuple(sorted(((a, b) for a in range(8) for b in range(8)), key=lambda o: -sum(min(v, 8 - v) for v in o)))
+CROSS = (2, 1, 3)
 
 
 def kernel(
@@ -20,8 +22,8 @@
     o_master, o_mom, o_m, o_s, o_model,
     terms, sib, master, drift, mom, mcode, scode, mscale, sscale,
     pairs, out_code, in_code, summed, old_m, old_s, weighted, part, mean, w_out, w_in, order, slice_out, slice_in,
-    s_in, s_sib, r_sib, s_code, r_code, s_w, r_w, s_part, r_part, s_mean, r_mean, s_slice, r_slice, s_block, r_block,
-    s_fwd, r_fwd,
+    sorted_rows, s_in, s_sib, r_sib, s_code, r_code, s_w, r_w, s_part, r_part, s_mean, r_mean, s_slice, r_slice,
+    s_block, r_block, s_fwd, r_fwd, near, far,
 ):
     g = lax.axis_index("group")
     f = lax.axis_index("fsdp")
@@ -43,6 +45,19 @@
         return pltpu.make_async_remote_copy(
             source, target, send, recv, device_id=device, device_id_type=MESH
         )
+
+    barrier = pltpu.get_barrier_semaphore()
+
+    def greet(device):
+        pl.semaphore_signal(barrier, inc=1, device_id=device, device_id_type=MESH)
+
+    pl.when(core == 1)(lambda: greet(sibling))
+    for d in RING:
+        greet(at(1 - xh, zs[d], 1))
+        if d:
+            greet(at(xh, zs[d], 1))
+    for dy, dx in PEERS:
+        greet((ys[dy] + xls[dx], f + 1 - core))
 
     loads = [
         pltpu.make_async_copy(grad.at[pl.ds(16 * k, 16)], terms.at[pl.ds(16 * k, 16)], s_in.at[k])
@@ -58,19 +73,31 @@
     for c in loads + small:
         c.start()
 
-    barrier = pltpu.get_barrier_semaphore()
-
-    def greet(device):
-        pl.semaphore_signal(barrier, inc=1, device_id=device, device_id_type=MESH)
-
-    for d in RING:
-        greet(at(1 - core, zs[d], xh))
-        greet(at(core, zs[d], 1 - core))
-        if d:
-            greet(at(core, zs[d], core))
-    pl.when(across == 1)(lambda: greet(at(core, z, core)))
-    for dy, dx in PEERS:
-        greet((ys[dy] + xls[dx], f))
+    for c in loads:
+        c.wait()
+
+    def tell(sem):
+        pl.semaphore_signal(sem, inc=1, device_id=sibling, device_id_type=MESH)
+
+    @pl.when(core == 0)
+    def _():
+        pl.semaphore_wait(barrier, 1)
+        tell(near)
+
+    @pl.when(core == 1)
+    def _():
+        pl.semaphore_wait(near, 1)
+
+    halves = [1 - z // 4, z // 4]
+
+    def half_rows(owner, k):
+        return pl.ds(pl.multiple_of(owner * 32 + halves[k] * 16, 16), 16)
+
+    swaps = [
+        remote(terms.at[half_rows(other, k)], sib.at[k], s_sib.at[k], r_sib.at[k], sibling) for k in range(2)
+    ]
+    for c in swaps:
+        c.start()
 
     for c in small[:4]:
         c.wait()
@@ -87,28 +114,6 @@
     old_m[...] = 0.9 * (signed * signed * signed * scale_of(mscale))
     unsigned = (scode[...].astype(F32) + 16.0) / 271.0
     old_s[...] = 0.999 * (unsigned * unsigned * scale_of(sscale))
-    for c in loads:
-        c.wait()
-
-    pl.semaphore_wait(barrier, 38 + across)
-
-    halves = [1 - z // 4, z // 4]
-
-    def half_rows(owner, k):
-        return pl.ds(pl.multiple_of(owner * 32 + halves[k] * 16, 16), 16)
-
-    swaps = [
-        remote(terms.at[half_rows(other, k)], sib.at[k], s_sib.at[k], r_sib.at[k], sibling) for k in range(2)
-    ]
-    for c in swaps:
-        c.start()
-
-    group_at = [ys[dy] + xls[dx] for dy, dx in PEERS]
-    group_from = [back_ys[dy] + xls[dx] for dy, dx in PEERS]
-    w_copies = [remote(w_out, w_in.at[i], s_w.at[i], r_w.at[i], (p, f)) for i, p in enumerate(group_at)]
-    for c in w_copies:
-        c.start()
-
     for k in range(2):
         swaps[k].wait_recv()
 
@@ -119,6 +124,17 @@
             return 0
 
         lax.fori_loop(0, 64, add_pair, 0, unroll=4)
+        if k == 0:
+
+            @pl.when(core == 1)
+            def _():
+                pl.semaphore_wait(barrier, 60)
+                tell(far)
+
+            @pl.when(core == 0)
+            def _():
+                pl.semaphore_wait(far, 1)
+
         for q in range(4):
             pz = halves[k] * 4 + q
             ahead = lax.rem(pz - z + 8, 8)
@@ -142,6 +158,13 @@
                     def _(n=n):
                         in_code[0] = out_code[n]
 
+    group_at = [(ys[dy] + xls[dx], xls[dx] * 8 + ys[dy] // 2) for dy, dx in PEERS]
+    group_from = [xls[dx] * 8 + back_ys[dy] // 2 for dy, dx in PEERS]
+    own_eight = xl * 8 + y
+    w_copies = [remote(w_out, w_in.at[i], s_w.at[i], r_w.at[i], (p, f)) for i, (p, _) in enumerate(group_at)]
+    for c in w_copies:
+        c.start()
+
     def code_wait(slot):
         remote(out_code.at[0], in_code.at[slot], s_code.at[0], r_code.at[slot], sibling).wait_recv()
 
@@ -173,8 +196,8 @@
         return pl.ds(pl.multiple_of(p * 8, 8), 8)
 
     part_copies = [
-        remote(weighted.at[eight(p)], part.at[i], s_part.at[i], r_part.at[i], (p, f))
-        for i, p in enumerate(group_at)
+        remote(weighted.at[eight(e)], part.at[i], s_part.at[i], r_part.at[i], (p, f))
+        for i, (p, e) in enumerate(group_at)
     ]
     for c in part_copies:
         c.start()
@@ -184,7 +207,7 @@
     for i in range(15):
         w_copies[i].wait_recv()
         all_weights = all_weights + w_in[i]
-    own_sum = weighted[eight(g), :]
+    own_sum = weighted[eight(own_eight), :]
     for i in range(15):
         part_copies[i].wait_recv()
         own_sum = own_sum + part[i]
@@ -194,86 +217,67 @@
         momentum = 0.9 * mom[at_rows, :] + mean_pseudo
         return master[at_rows, :] - 0.7 * (mean_pseudo + 0.9 * momentum), momentum
 
-    fresh, _ = nesterov(eight(g), own_mean)
+    fresh, _ = nesterov(eight(own_eight), own_mean)
     order[...] = fresh
-    slice_out[0:4, :] = order[pl.ds(0, 4, stride=2), :]
-    slice_out[4:8, :] = order[pl.ds(1, 4, stride=2), :]
-    mean[eight(g), :] = own_mean
+    two = [order[pl.ds(r, 4, stride=2), :] for r in range(2)]
+    slice_out[0] = jnp.concatenate(two, axis=0).astype(BF16)
+    mean[eight(own_eight), :] = own_mean
+    half = z // 4
+    where = y * 8 + lax.rem(z, 4) * 2 + core
     slice_copies = []
-    for d in RING:
-        for dx in (1, 0):
-            slot = ((8 - d) % 8) * 2
-            to = at((xh + dx) % 2, zs[d], xh)
-            n = d * 2 + dx
-            where = z * 2 + core
-            copy = remote(slice_out, slice_in.at[where], s_slice.at[n], r_slice.at[where], to)
-            slice_copies.append(copy)
-            if d or dx:
-                copy.start()
-            else:
-                pl.when(xh != core)(copy.start)
-
-                @pl.when(xh == core)
-                def _():
-                    slice_in[where] = slice_out[...]
+    for n, (dy, dz) in enumerate(PLANE):
+        to = (ys[dy] + xl, xh * 16 + zs[dz] * 2 + half)
+        copy = remote(slice_out.at[0], slice_in.at[where], s_slice.at[n], r_slice.at[where], to)
+        slice_copies.append(copy)
+        if n < 63:
+            copy.start()
+        else:
+            pl.when(half != core)(copy.start)
+            keep = pltpu.make_async_copy(slice_out.at[0], slice_in.at[where], r_slice.at[where])
+            pl.when(half == core)(keep.start)
 
     mean_copies = []
-    for i, p in enumerate(group_at):
-        c = remote(mean.at[eight(g)], mean.at[eight(g)], s_mean.at[i], r_mean.at[i], (p, f))
+    mine = mean.at[eight(own_eight)]
+    for i, (p, _) in enumerate(group_at):
+        c = remote(mine, mine, s_mean.at[i], r_mean.at[i], (p, f))
         c.start()
         mean_copies.append(c)
 
-    def slice_wait(where):
-        remote(slice_out, slice_in.at[where], s_slice.at[0], r_slice.at[where], sibling).wait_recv()
-
-    for k in range(8):
-        for pc in range(2):
-            stays = (xh == core) & (z == k) & (core == pc)
-            pl.when(jnp.logical_not(stays))(lambda w=k * 2 + pc: slice_wait(w))
-    mine = pl.ds(pl.multiple_of(core * 32, 32), 32)
-    flat = slice_in.reshape(128, 128)
-
-    def columns_of(p):
-        return pl.ds(pl.multiple_of(p * 512, 512), 512)
-
-    for k in range(2):
+    x = xh * 2 + xl
+    xs = [lax.rem(x + d, 4) for d in range(4)]
+
+    def block(source_x, source_core, d):
+        row = (source_x // 2 * 2 + source_core) * 16
+        column = (lax.rem(source_x, 2) * 8 + ys[d] // 2) * 512
+        return o_model.at[pl.ds(pl.multiple_of(row, 16), 16), pl.ds(pl.multiple_of(column, 512), 512)]
+
+    sends = []
+    for n, d in enumerate(reversed(RING)):
+        from_y = ys[d] // 2
+        for k in range(8):
+            slot = from_y * 8 + k
+            remote(slice_out.at[0], slice_in.at[slot], s_slice.at[0], r_slice.at[slot], sibling).wait_recv()
+        wide = slice_in[pl.ds(pl.multiple_of(from_y * 8, 8), 8)].astype(F32)
+        sorted_rows[...] = wide.reshape(64, 128)
+        piece = block(x, core, d)
         for j in range(4):
-            two = [flat[pl.ds((k * 16 + h * 8) * 4 + j, 8, stride=4), :] for h in range(2)]
-            o_model[
-                pl.ds(pl.multiple_of(core * 32 + k * 16, 16), 16),
-                pl.ds(pl.multiple_of(g * 512 + j * 128, 128), 128),
-            ] = jnp.concatenate(two, axis=0).astype(BF16)
-
-    def block(p):
-        return o_model.at[mine, columns_of(p)]
-
-    block_copies = [
-        remote(block(g), block(g), s_block.at[i], r_block.at[i], (p, f)) for i, p in enumerate(group_at)
-    ]
-    for c in block_copies:
-        c.start()
-    fwd = [remote(block(g), block(g), s_fwd.at[15], r_fwd.at[15], sibling)]
-    fwd[0].start()
-
-    for i, p in enumerate(group_from):
-        remote(mean.at[eight(p)], mean.at[eight(p)], s_mean.at[i], r_mean.at[i], sibling).wait_recv()
+            two = [sorted_rows[pl.ds(h * 32 + j, 8, stride=4), :] for h in range(2)]
+            piece[:, j * 128 : j * 128 + 128] = jnp.concatenate(two, axis=0).astype(BF16)
+        for dx in CROSS:
+            to = (y * 2 + lax.rem(xs[dx], 2), xs[dx] // 2 * 16 + z * 2 + core)
+            sends.append(remote(piece, piece, s_block.at[dx * 8 + n], r_block.at[dx * 8 + n], to))
+            sends[-1].start()
+        sends.append(remote(piece, piece, s_fwd.at[n], r_fwd.at[n], sibling))
+        sends[-1].start()
+
+    for i, e in enumerate(group_from):
+        remote(mean.at[eight(e)], mean.at[eight(e)], s_mean.at[i], r_mean.at[i], sibling).wait_recv()
     everything = pl.ds(0, 128)
     o_master[...], o_mom[...] = nesterov(everything, mean[...])
 
-    for i, p in enumerate(group_from):
-        remote(block(p), block(p), s_block.at[i], r_block.at[i], sibling).wait_recv()
-        c = remote(block(p), block(p), s_fwd.at[i], r_fwd.at[i], sibling)
-        c.start()
-        fwd.append(c)
-
-    theirs = pl.ds(pl.multiple_of(other * 32, 32), 32)
-    for i, p in enumerate(group_from + [g]):
-        there = o_model.at[theirs, columns_of(p)]
-        remote(there, there, s_fwd.at[i], r_fwd.at[i], sibling).wait_recv()
-
-    for c in swaps + w_copies + part_copies + mean_copies + block_copies + fwd + slice_copies[:15]:
+    for c in swaps + w_copies + part_copies + mean_copies + slice_copies[:63]:
         c.wait_send()
-    pl.when(xh != core)(slice_copies[15].wait_send)
+    pl.when(half != core)(slice_copies[63].wait_send)
     for n in range(16):
         k, q, pc = n // 8, n // 2 % 4, n % 2
         ahead = lax.rem(halves[k] * 4 + q - z + 8, 8)
@@ -283,6 +287,21 @@
             done.wait_send()
         else:
             pl.when(jnp.logical_not(stays))(done.wait_send)
+
+    for n, d in enumerate(reversed(RING)):
+        for dx in CROSS:
+            piece = block(xs[4 - dx], core, d)
+            at_n = dx * 8 + n
+            remote(piece, piece, s_block.at[at_n], r_block.at[at_n], sibling).wait_recv()
+            sends.append(remote(piece, piece, s_fwd.at[at_n], r_fwd.at[at_n], sibling))
+            sends[-1].start()
+    for n, d in enumerate(reversed(RING)):
+        for dx in (0,) + CROSS:
+            piece = block(xs[(4 - dx) % 4], other, d)
+            at_n = dx * 8 + n
+            remote(piece, piece, s_fwd.at[at_n], r_fwd.at[at_n], sibling).wait_recv()
+    for c in sends:
+        c.wait_send()
 
 
 def outer_step(*args):
@@ -303,9 +322,11 @@
             square, square, square, codes, codes, pltpu.VMEM((1, 2, 32), F32), pltpu.VMEM((1, 2, 32), F32),
             pltpu.VMEM((1024, 128), F32), pltpu.VMEM((16, 128, 128), jnp.int16), pltpu.VMEM((16, 128, 128), jnp.int16),
             square, square, square, square, eight(15), square,
-            pltpu.VMEM((8, 128), F32), eight(15), pltpu.VMEM((8, 128), F32), pltpu.VMEM((8, 128), F32), eight(16),
+            pltpu.VMEM((8, 128), F32), eight(15), pltpu.VMEM((8, 128), F32),
+            pltpu.VMEM((1, 8, 128), BF16), pltpu.VMEM((64, 8, 128), BF16), pltpu.VMEM((64, 128), F32),
             dma((11,)), dma((2,)), dma((2,)), dma((16,)), dma((16,)), dma((15,)), dma((15,)), dma((15,)), dma((15,)),
-            dma((15,)), dma((15,)), dma((16,)), dma((16,)), dma((15,)), dma((15,)), dma((16,)), dma((16,)),
+            dma((15,)), dma((15,)), dma((64,)), dma((64,)), dma((32,)), dma((32,)), dma((32,)), dma((32,)),
+            pltpu.SemaphoreType.REGULAR, pltpu.SemaphoreType.REGULAR,
         ],
         compiler_params=pltpu.CompilerParams(
             collective_id=0, has_side_effects=True, vmem_limit_bytes=16 * 1024 * 1024

time: 62.2 us -> 57.5 us (0.924)
  Pallas kernels: 60.7 us -> 56.1 us
    pallas_call x1, Pallas kernels: 59.6 us -> 55 us  [outer_step(): pl.pallas_call(kernel, out_shape=(out, out, out, out, pltpu.VMEM((64, 819...]
where the time goes in v3:
time: 57.5 us; the launch traced here: 57.4 us
  Pallas kernels  56.1 us (98%)
  between operations  1.29 us (2%)
    pallas_call x1, Pallas kernels, outer_step(): pl.pallas_call(kernel, out_shape=(out, out, out, out, pltpu.VMEM((64, 819...  55 us

profile of v3, /device:TPU:1, one launch (start us, length us, event | category | flops | bytes accessed | tf_op | source)
XLA Modules:
  0.0 57.4 jit_solution(12676723540795779469)
XLA Ops:
  1.3 55.0 %outer_step.1 = (f32[128,128]{1,0:T(8,128)S(1)}, f32[128,128]{1,0:T(8,128)S(1)}, f32[128,128]{1,0:T(8,128)S(1)}, f32[128,128]{1,0:T(8,128)S(1)}, bf16[64,8192]{1,0:T(8,128)(2,1)S(1)}) custom-call(bf16[64,8192]{1,0:T(8,128)(2,1)} %bitcast.46, f32[128,128]{1,0:T(8,128)} %bitcast.47, f32[128,128]{1,0:T(8,128)} %bitcast.48, f32[128,128]{1,0:T(8,128)} %bitcast.49, ...), custom_call_target="tpu_custom_call" | custom-call | tf_op jit(solution)/shard_map/outer_step/pallas_call | solution.py:315
  56.3 1.1 %hand_over.1 = (f32[128,128]{1,0:T(8,128)}, f32[128,128]{1,0:T(8,128)}, f32[128,128]{1,0:T(8,128)}, f32[128,128]{1,0:T(8,128)}, bf16[64,8192]{1,0:T(8,128)(2,1)}) custom-call(f32[128,128]{1,0:T(8,128)S(1)} %get-tuple-element.15.refs_0_, f32[128,128]{1,0:T(8,128)S(1)} %get-tuple-element.16.refs_1_, f32[128,128]{1,0:T(8,128)S(1)} %get-tuple-element.17.refs_2_, ...), custom_call_target="tpu_custom_call" | custom-call | tf_op jit(solution)/shard_map/hand_over/pallas_call | solution.py:359

commit v4 on v3

--- a/solution.py
+++ b/solution.py
@@ -21,8 +21,8 @@
     grad, master_in, drift_in, mom_in, mcode_in, scode_in, mscale_in, sscale_in, counts,
     o_master, o_mom, o_m, o_s, o_model,
     terms, sib, master, drift, mom, mcode, scode, mscale, sscale,
-    pairs, out_code, in_code, summed, old_m, old_s, weighted, part, mean, w_out, w_in, order, slice_out, slice_in,
-    sorted_rows, s_in, s_sib, r_sib, s_code, r_code, s_w, r_w, s_part, r_part, s_mean, r_mean, s_slice, r_slice,
+    wide, by_owner, cross_code, out_code, x_code, in_code, summed, old_m, old_s, weighted, part, mean, w_out, w_in, order, slice_out, slice_in,
+    sorted_rows, s_in, s_sib, r_sib, s_code, r_code, s_x, r_x, s_w, r_w, s_part, r_part, s_mean, r_mean, s_slice, r_slice,
     s_block, r_block, s_fwd, r_fwd, near, far,
 ):
     g = lax.axis_index("group")
@@ -30,7 +30,6 @@
     y, xl = g // 2, g % 2
     xh, z, core = f // 16, (f // 2) % 8, f % 2
     other = 1 - core
-    across = (xh + core) % 2
     zs = [lax.rem(z + d, 8) for d in range(8)]
     ys = [lax.rem(y + d, 8) * 2 for d in range(8)]
     back_ys = [lax.rem(y + 8 - d, 8) * 2 for d in range(8)]
@@ -53,15 +52,18 @@
 
     pl.when(core == 1)(lambda: greet(sibling))
     for d in RING:
-        greet(at(1 - xh, zs[d], 1))
-        if d:
-            greet(at(xh, zs[d], 1))
+        greet(at(xh, zs[d], 1) if d else at(1 - xh, z, 1))
     for dy, dx in PEERS:
         greet((ys[dy] + xls[dx], f + 1 - core))
 
+    z_half = z // 4
+    tiles = [px * 2 + pz for px in (1 - xh, xh) for pz in (1 - z_half, z_half)]
+
+    def sixteen(t):
+        return pl.ds(pl.multiple_of(t * 16, 16), 16)
+
     loads = [
-        pltpu.make_async_copy(grad.at[pl.ds(16 * k, 16)], terms.at[pl.ds(16 * k, 16)], s_in.at[k])
-        for k in range(4)
+        pltpu.make_async_copy(grad.at[sixteen(t)], terms.at[sixteen(t)], s_in.at[k]) for k, t in enumerate(tiles)
     ]
     small = [
         pltpu.make_async_copy(a, b, s_in.at[4 + k])
@@ -73,8 +75,31 @@
     for c in loads + small:
         c.start()
 
-    for c in loads:
-        c.wait()
+    def regroup(k):
+        loads[k].wait()
+
+        def widen(j, _):
+            columns = pl.ds(pl.multiple_of(j * 128, 128), 128)
+            wide[pl.ds(pl.multiple_of(j * 16, 16), 16), :] = terms[sixteen(tiles[k]), columns].astype(F32)
+            return 0
+
+        lax.fori_loop(0, 64, widen, 0, unroll=4)
+        for q in range(4):
+            for pc in range(2):
+                for big in range(8):
+                    two = [wide[pl.ds(big * 128 + q * 4 + pc * 2 + r, 8, stride=16), :] for r in range(2)]
+                    by_owner[pc, tiles[k] * 4 + q, big * 16 : big * 16 + 16, :] = jnp.concatenate(two, axis=0).astype(
+                        BF16
+                    )
+
+    def four(t):
+        return pl.ds(t * 4, 4)
+
+    swaps = [
+        remote(by_owner.at[other, four(t)], sib.at[four(t)], s_sib.at[k], r_sib.at[k], sibling)
+        for k, t in enumerate(tiles)
+    ]
+    regroup(0)
 
     def tell(sem):
         pl.semaphore_signal(sem, inc=1, device_id=sibling, device_id_type=MESH)
@@ -88,16 +113,10 @@
     def _():
         pl.semaphore_wait(near, 1)
 
-    halves = [1 - z // 4, z // 4]
-
-    def half_rows(owner, k):
-        return pl.ds(pl.multiple_of(owner * 32 + halves[k] * 16, 16), 16)
-
-    swaps = [
-        remote(terms.at[half_rows(other, k)], sib.at[k], s_sib.at[k], r_sib.at[k], sibling) for k in range(2)
-    ]
-    for c in swaps:
-        c.start()
+    swaps[0].start()
+    for k in range(1, 4):
+        regroup(k)
+        swaps[k].start()
 
     for c in small[:4]:
         c.wait()
@@ -114,49 +133,54 @@
     old_m[...] = 0.9 * (signed * signed * signed * scale_of(mscale))
     unsigned = (scode[...].astype(F32) + 16.0) / 271.0
     old_s[...] = 0.999 * (unsigned * unsigned * scale_of(sscale))
+
+    @pl.when(core == 1)
+    def _():
+        pl.semaphore_wait(barrier, 46)
+        tell(far)
+
+    @pl.when(core == 0)
+    def _():
+        pl.semaphore_wait(far, 1)
+
+    def pair(chip):
+        return by_owner[core, chip].astype(F32) + sib[chip].astype(F32)
+
+    def to_codes(values):
+        return jnp.round(values).astype(jnp.int32).astype(jnp.int16)
+
+    crossing = []
     for k in range(2):
         swaps[k].wait_recv()
-
-        def add_pair(j, _, k=k):
-            columns = pl.ds(pl.multiple_of(j * 128, 128), 128)
-            both = terms[half_rows(core, k), columns].astype(F32) + sib[k, :, columns].astype(F32)
-            pairs[pl.ds(pl.multiple_of(j * 16, 16), 16), :] = both * CODE
-            return 0
-
-        lax.fori_loop(0, 64, add_pair, 0, unroll=4)
-        if k == 0:
-
-            @pl.when(core == 1)
-            def _():
-                pl.semaphore_wait(barrier, 60)
-                tell(far)
-
-            @pl.when(core == 0)
-            def _():
-                pl.semaphore_wait(far, 1)
-
         for q in range(4):
-            pz = halves[k] * 4 + q
-            ahead = lax.rem(pz - z + 8, 8)
-            slot = across * 8 + ahead
-            for pc in range(2):
-                n = k * 8 + q * 2 + pc
-                for big in range(8):
-                    two = [pairs[pl.ds(big * 128 + q * 4 + pc * 2 + r, 8, stride=16), :] for r in range(2)]
-                    whole = jnp.round(jnp.concatenate(two, axis=0)).astype(jnp.int32)
-                    out_code[n, big * 16 : big * 16 + 16, :] = whole.astype(jnp.int16)
-                copy = remote(
-                    out_code.at[n], in_code.at[slot], s_code.at[n], r_code.at[slot], at(core, pz, pc)
-                )
-                if k == 0:
-                    copy.start()
-                else:
-                    stays = (ahead == 0) & (across == 0) & (core == pc)
-                    pl.when(jnp.logical_not(stays))(copy.start)
-
-                    @pl.when(stays)
-                    def _(n=n):
-                        in_code[0] = out_code[n]
+            pz = lax.rem(tiles[k], 2) * 4 + q
+            cross_code[pz] = to_codes(pair(tiles[k] * 4 + q) * CODE)
+            c = remote(cross_code.at[pz], x_code.at[pz], s_x.at[k * 4 + q], r_x.at[pz], at(1 - xh, z, core))
+            c.start()
+            crossing.append(c)
+
+    along = []
+    for k in range(2):
+        swaps[2 + k].wait_recv()
+        for q in range(4):
+            pz = lax.rem(tiles[2 + k], 2) * 4 + q
+            mine = pair(tiles[2 + k] * 4 + q) * CODE
+            remote(x_code.at[pz], x_code.at[pz], s_x.at[0], r_x.at[pz], sibling).wait_recv()
+            both = to_codes(0.5 * (mine + x_code[pz].astype(F32)))
+            c = remote(out_code.at[pz], in_code.at[z], s_code.at[k * 4 + q], r_code.at[z], at(xh, pz, core))
+            along.append(c)
+            if k == 0:
+                out_code[pz] = both
+                c.start()
+            else:
+                @pl.when(lax.rem(z, 4) == q)
+                def _(both=both):
+                    in_code[z] = both
+
+                @pl.when(lax.rem(z, 4) != q)
+                def _(both=both, c=c, pz=pz):
+                    out_code[pz] = both
+                    c.start()
 
     group_at = [(ys[dy] + xls[dx], xls[dx] * 8 + ys[dy] // 2) for dy, dx in PEERS]
     group_from = [xls[dx] * 8 + back_ys[dy] // 2 for dy, dx in PEERS]
@@ -165,19 +189,12 @@
     for c in w_copies:
         c.start()
 
-    def code_wait(slot):
-        remote(out_code.at[0], in_code.at[slot], s_code.at[0], r_code.at[slot], sibling).wait_recv()
-
     total = jnp.zeros((128, 128), jnp.int32)
-    for d in RING:
-        for dx in range(2):
-            slot = dx * 8 + d
-            if slot:
-                code_wait(slot)
-            else:
-                pl.when(xh != core)(lambda: code_wait(0))
-            total = total + in_code[slot].astype(jnp.int32)
-    total = total.astype(F32) * (1.0 / CODE)
+    for slot in range(8):
+        c = remote(out_code.at[slot], in_code.at[slot], s_code.at[0], r_code.at[slot], sibling)
+        pl.when(slot != z)(c.wait_recv)
+        total = total + in_code[slot].astype(jnp.int32)
+    total = total.astype(F32) * (2.0 / CODE)
     for big in range(8):
         for r in range(2):
             summed[pl.ds(big * 16 + r, 8, stride=2), :] = total[big * 16 + r * 8 : big * 16 + r * 8 + 8]
@@ -222,24 +239,23 @@
     two = [order[pl.ds(r, 4, stride=2), :] for r in range(2)]
     slice_out[0] = jnp.concatenate(two, axis=0).astype(BF16)
     mean[eight(own_eight), :] = own_mean
-    half = z // 4
     where = y * 8 + lax.rem(z, 4) * 2 + core
     slice_copies = []
     for n, (dy, dz) in enumerate(PLANE):
-        to = (ys[dy] + xl, xh * 16 + zs[dz] * 2 + half)
+        to = (ys[dy] + xl, xh * 16 + zs[dz] * 2 + z_half)
         copy = remote(slice_out.at[0], slice_in.at[where], s_slice.at[n], r_slice.at[where], to)
         slice_copies.append(copy)
         if n < 63:
             copy.start()
         else:
-            pl.when(half != core)(copy.start)
+            pl.when(z_half != core)(copy.start)
             keep = pltpu.make_async_copy(slice_out.at[0], slice_in.at[where], r_slice.at[where])
-            pl.when(half == core)(keep.start)
+            pl.when(z_half == core)(keep.start)
 
     mean_copies = []
-    mine = mean.at[eight(own_eight)]
+    own_rows = mean.at[eight(own_eight)]
     for i, (p, _) in enumerate(group_at):
-        c = remote(mine, mine, s_mean.at[i], r_mean.at[i], (p, f))
+        c = remote(own_rows, own_rows, s_mean.at[i], r_mean.at[i], (p, f))
         c.start()
         mean_copies.append(c)
 
@@ -257,8 +273,8 @@
         for k in range(8):
             slot = from_y * 8 + k
             remote(slice_out.at[0], slice_in.at[slot], s_slice.at[0], r_slice.at[slot], sibling).wait_recv()
-        wide = slice_in[pl.ds(pl.multiple_of(from_y * 8, 8), 8)].astype(F32)
-        sorted_rows[...] = wide.reshape(64, 128)
+        arrived = slice_in[pl.ds(pl.multiple_of(from_y * 8, 8), 8)].astype(F32)
+        sorted_rows[...] = arrived.reshape(64, 128)
         piece = block(x, core, d)
         for j in range(4):
             two = [sorted_rows[pl.ds(h * 32 + j, 8, stride=4), :] for h in range(2)]
@@ -275,18 +291,12 @@
     everything = pl.ds(0, 128)
     o_master[...], o_mom[...] = nesterov(everything, mean[...])
 
-    for c in swaps + w_copies + part_copies + mean_copies + slice_copies[:63]:
+    for c in swaps + crossing + w_copies + part_copies + mean_copies + slice_copies[:63]:
         c.wait_send()
-    pl.when(half != core)(slice_copies[63].wait_send)
-    for n in range(16):
-        k, q, pc = n // 8, n // 2 % 4, n % 2
-        ahead = lax.rem(halves[k] * 4 + q - z + 8, 8)
-        done = remote(out_code.at[n], in_code.at[0], s_code.at[n], r_code.at[0], sibling)
-        stays = (ahead == 0) & (across == 0) & (core == pc)
-        if k == 0:
-            done.wait_send()
-        else:
-            pl.when(jnp.logical_not(stays))(done.wait_send)
+    pl.when(z_half != core)(slice_copies[63].wait_send)
+    for q in range(4):
+        along[q].wait_send()
+        pl.when(lax.rem(z, 4) != q)(along[4 + q].wait_send)
 
     for n, d in enumerate(reversed(RING)):
         for dx in CROSS:
@@ -309,6 +319,7 @@
     vmem = pl.BlockSpec(memory_space=pltpu.VMEM)
     square = pltpu.VMEM((128, 128), F32)
     codes = pltpu.VMEM((128, 128), jnp.int32)
+    codes16 = pltpu.VMEM((8, 128, 128), jnp.int16)
     eight = lambda n: pltpu.VMEM((n, 8, 128), F32)
     dma = pltpu.SemaphoreType.DMA
     out = pltpu.VMEM((128, 128), F32)
@@ -318,14 +329,14 @@
         in_specs=[hbm] * 8 + [pl.BlockSpec(memory_space=pltpu.SMEM)],
         out_specs=(vmem,) * 5,
         scratch_shapes=[
-            pltpu.VMEM((64, 8192), BF16), pltpu.VMEM((2, 16, 8192), BF16),
+            pltpu.VMEM((64, 8192), BF16), pltpu.VMEM((16, 128, 128), BF16),
             square, square, square, codes, codes, pltpu.VMEM((1, 2, 32), F32), pltpu.VMEM((1, 2, 32), F32),
-            pltpu.VMEM((1024, 128), F32), pltpu.VMEM((16, 128, 128), jnp.int16), pltpu.VMEM((16, 128, 128), jnp.int16),
+            pltpu.VMEM((1024, 128), F32), pltpu.VMEM((2, 16, 128, 128), BF16), codes16, codes16, codes16, codes16,
             square, square, square, square, eight(15), square,
             pltpu.VMEM((8, 128), F32), eight(15), pltpu.VMEM((8, 128), F32),
             pltpu.VMEM((1, 8, 128), BF16), pltpu.VMEM((64, 8, 128), BF16), pltpu.VMEM((64, 128), F32),
-            dma((11,)), dma((2,)), dma((2,)), dma((16,)), dma((16,)), dma((15,)), dma((15,)), dma((15,)), dma((15,)),
-            dma((15,)), dma((15,)), dma((64,)), dma((64,)), dma((32,)), dma((32,)), dma((32,)), dma((32,)),
+            dma((11,)), dma((4,)), dma((4,)), dma((8,)), dma((8,)), dma((8,)), dma((8,)), dma((15,)), dma((15,)), dma((15,)),
+            dma((15,)), dma((15,)), dma((15,)), dma((64,)), dma((64,)), dma((32,)), dma((32,)), dma((32,)), dma((32,)),
             pltpu.SemaphoreType.REGULAR, pltpu.SemaphoreType.REGULAR,
         ],
         compiler_params=pltpu.CompilerParams(

time: 57.5 us -> 53.9 us (0.937)
  Pallas kernels: 56.1 us -> 52.4 us
    pallas_call x1, Pallas kernels: 55 us -> 51.4 us  [outer_step(): pl.pallas_call(kernel, out_shape=(out, out, out, out, pltpu.VMEM((64, 819...]
where the time goes in v4:
time: 53.9 us; the launch traced here: 53.7 us
  Pallas kernels  52.4 us (97%)
  between operations  1.29 us (2%)
    pallas_call x1, Pallas kernels, outer_step(): pl.pallas_call(kernel, out_shape=(out, out, out, out, pltpu.VMEM((64, 819...  51.4 us
    pallas_call x1, Pallas kernels, on_device(): pl.pallas_call(hand_over, out_shape=tuple((jax.ShapeDtypeStruct(o.shape,...  1.08 us

profile of v4, /device:TPU:1, one launch (start us, length us, event | category | flops | bytes accessed | tf_op | source)
XLA Modules:
  0.0 53.7 jit_solution(9880828077489971348)
XLA Ops:
  1.3 51.4 %outer_step.1 = (f32[128,128]{1,0:T(8,128)S(1)}, f32[128,128]{1,0:T(8,128)S(1)}, f32[128,128]{1,0:T(8,128)S(1)}, f32[128,128]{1,0:T(8,128)S(1)}, bf16[64,8192]{1,0:T(8,128)(2,1)S(1)}) custom-call(bf16[64,8192]{1,0:T(8,128)(2,1)} %bitcast.46, f32[128,128]{1,0:T(8,128)} %bitcast.47, f32[128,128]{1,0:T(8,128)} %bitcast.48, f32[128,128]{1,0:T(8,128)} %bitcast.49, ...), custom_call_target="tpu_custom_call" | custom-call | tf_op jit(solution)/shard_map/outer_step/pallas_call | solution.py:326
  52.6 1.1 %hand_over.1 = (f32[128,128]{1,0:T(8,128)}, f32[128,128]{1,0:T(8,128)}, f32[128,128]{1,0:T(8,128)}, f32[128,128]{1,0:T(8,128)}, bf16[64,8192]{1,0:T(8,128)(2,1)}) custom-call(f32[128,128]{1,0:T(8,128)S(1)} %get-tuple-element.15.refs_0_, f32[128,128]{1,0:T(8,128)S(1)} %get-tuple-element.16.refs_1_, f32[128,128]{1,0:T(8,128)S(1)} %get-tuple-element.17.refs_2_, ...), custom_call_target="tpu_custom_call" | custom-call | tf_op jit(solution)/shard_map/hand_over/pallas_call | solution.py:370

commit v5 on v4

--- a/solution.py
+++ b/solution.py
@@ -13,7 +13,7 @@
 CODE = 27408.0
 RING = (4, 3, 5, 2, 6, 1, 7, 0)
 PEERS = tuple((dy, dx) for dy in RING for dx in (1, 0))[:15]
-PLANE = tuple(sorted(((a, b) for a in range(8) for b in range(8)), key=lambda o: -sum(min(v, 8 - v) for v in o)))
+PLANE = tuple((dy, dz) for dy in reversed(RING) for dz in RING if dy or dz)
 CROSS = (2, 1, 3)
 
 
@@ -50,12 +50,9 @@
     def greet(device):
         pl.semaphore_signal(barrier, inc=1, device_id=device, device_id_type=MESH)
 
+    across_x = at(1 - xh, z, core)
+    greet(at(1 - xh, z, 0))
     pl.when(core == 1)(lambda: greet(sibling))
-    for d in RING:
-        greet(at(xh, zs[d], 1) if d else at(1 - xh, z, 1))
-    for dy, dx in PEERS:
-        greet((ys[dy] + xls[dx], f + 1 - core))
-
     z_half = z // 4
     tiles = [px * 2 + pz for px in (1 - xh, xh) for pz in (1 - z_half, z_half)]
 
@@ -92,31 +89,47 @@
                         BF16
                     )
 
-    def four(t):
-        return pl.ds(t * 4, 4)
-
+    for k in range(4):
+        regroup(k)
+
+    chips = [(1 - xh) * 8 + zs[d] for d in RING] + [xh * 8 + zs[d] for d in RING]
     swaps = [
-        remote(by_owner.at[other, four(t)], sib.at[four(t)], s_sib.at[k], r_sib.at[k], sibling)
-        for k, t in enumerate(tiles)
+        remote(by_owner.at[other, chip], sib.at[k], s_sib.at[k], r_sib.at[k], sibling)
+        for k, chip in enumerate(chips)
     ]
-    regroup(0)
 
     def tell(sem):
         pl.semaphore_signal(sem, inc=1, device_id=sibling, device_id_type=MESH)
 
     @pl.when(core == 0)
     def _():
-        pl.semaphore_wait(barrier, 1)
+        pl.semaphore_wait(barrier, 3)
         tell(near)
 
     @pl.when(core == 1)
     def _():
         pl.semaphore_wait(near, 1)
 
-    swaps[0].start()
-    for k in range(1, 4):
-        regroup(k)
-        swaps[k].start()
+    for c in swaps:
+        c.start()
+    for d in RING[:7]:
+        greet(at(xh, zs[d], 1))
+    for dy, dx in PEERS:
+        greet((ys[dy] + xls[dx], f + 1 - core))
+
+    def pair(k):
+        swaps[k].wait_recv()
+        return by_owner[core, chips[k]].astype(F32) + sib[k].astype(F32)
+
+    def to_codes(values):
+        return jnp.round(values).astype(jnp.int32).astype(jnp.int16)
+
+    crossing = []
+    for k, d in enumerate(RING):
+        cross_code[d] = to_codes(pair(k) * CODE)
+        c = remote(cross_code.at[d], x_code.at[d], s_x.at[d], r_x.at[d], across_x)
+        c.start()
+        crossing.append(c)
 
     for c in small[:4]:
         c.wait()
@@ -136,51 +149,24 @@
 
     @pl.when(core == 1)
     def _():
-        pl.semaphore_wait(barrier, 46)
+        pl.semaphore_wait(barrier, 44)
         tell(far)
 
     @pl.when(core == 0)
     def _():
         pl.semaphore_wait(far, 1)
 
-    def pair(chip):
-        return by_owner[core, chip].astype(F32) + sib[chip].astype(F32)
-
-    def to_codes(values):
-        return jnp.round(values).astype(jnp.int32).astype(jnp.int16)
-
-    crossing = []
-    for k in range(2):
-        swaps[k].wait_recv()
-        for q in range(4):
-            pz = lax.rem(tiles[k], 2) * 4 + q
-            cross_code[pz] = to_codes(pair(tiles[k] * 4 + q) * CODE)
-            c = remote(cross_code.at[pz], x_code.at[pz], s_x.at[k * 4 + q], r_x.at[pz], at(1 - xh, z, core))
+    along = []
+    for k, d in enumerate(RING):
+        own = pair(8 + k) * CODE
+        crossing[k].wait_recv()
+        both = own + x_code[d].astype(F32)
+        if d:
+            out_code[d] = to_codes(0.5 * both)
+            c = remote(out_code.at[d], in_code.at[d], s_code.at[d], r_code.at[d], at(xh, zs[d], core))
             c.start()
-            crossing.append(c)
-
-    along = []
-    for k in range(2):
-        swaps[2 + k].wait_recv()
-        for q in range(4):
-            pz = lax.rem(tiles[2 + k], 2) * 4 + q
-            mine = pair(tiles[2 + k] * 4 + q) * CODE
-            remote(x_code.at[pz], x_code.at[pz], s_x.at[0], r_x.at[pz], sibling).wait_recv()
-            both = to_codes(0.5 * (mine + x_code[pz].astype(F32)))
-            c = remote(out_code.at[pz], in_code.at[z], s_code.at[k * 4 + q], r_code.at[z], at(xh, pz, core))
             along.append(c)
-            if k == 0:
-                out_code[pz] = both
-                c.start()
-            else:
-                @pl.when(lax.rem(z, 4) == q)
-                def _(both=both):
-                    in_code[z] = both
-
-                @pl.when(lax.rem(z, 4) != q)
-                def _(both=both, c=c, pz=pz):
-                    out_code[pz] = both
-                    c.start()
+    kept = both * (1.0 / CODE)
 
     group_at = [(ys[dy] + xls[dx], xls[dx] * 8 + ys[dy] // 2) for dy, dx in PEERS]
     group_from = [xls[dx] * 8 + back_ys[dy] // 2 for dy, dx in PEERS]
@@ -190,11 +176,10 @@
         c.start()
 
     total = jnp.zeros((128, 128), jnp.int32)
-    for slot in range(8):
-        c = remote(out_code.at[slot], in_code.at[slot], s_code.at[0], r_code.at[slot], sibling)
-        pl.when(slot != z)(c.wait_recv)
-        total = total + in_code[slot].astype(jnp.int32)
-    total = total.astype(F32) * (2.0 / CODE)
+    for c, d in zip(along, RING):
+        c.wait_recv()
+        total = total + in_code[d].astype(jnp.int32)
+    total = total.astype(F32) * (2.0 / CODE) + kept
     for big in range(8):
         for r in range(2):
             summed[pl.ds(big * 16 + r, 8, stride=2), :] = total[big * 16 + r * 8 : big * 16 + r * 8 + 8]
@@ -241,7 +226,7 @@
     mean[eight(own_eight), :] = own_mean
     where = y * 8 + lax.rem(z, 4) * 2 + core
     slice_copies = []
-    for n, (dy, dz) in enumerate(PLANE):
+    for n, (dy, dz) in enumerate(PLANE + ((0, 0),)):
         to = (ys[dy] + xl, xh * 16 + zs[dz] * 2 + z_half)
         copy = remote(slice_out.at[0], slice_in.at[where], s_slice.at[n], r_slice.at[where], to)
         slice_copies.append(copy)
@@ -291,12 +276,9 @@
     everything = pl.ds(0, 128)
     o_master[...], o_mom[...] = nesterov(everything, mean[...])
 
-    for c in swaps + crossing + w_copies + part_copies + mean_copies + slice_copies[:63]:
+    for c in swaps + crossing + along + w_copies + part_copies + mean_copies + slice_copies[:63]:
         c.wait_send()
     pl.when(z_half != core)(slice_copies[63].wait_send)
-    for q in range(4):
-        along[q].wait_send()
-        pl.when(lax.rem(z, 4) != q)(along[4 + q].wait_send)
 
     for n, d in enumerate(reversed(RING)):
         for dx in CROSS:
@@ -335,7 +317,7 @@
             square, square, square, square, eight(15), square,
             pltpu.VMEM((8, 128), F32), eight(15), pltpu.VMEM((8, 128), F32),
             pltpu.VMEM((1, 8, 128), BF16), pltpu.VMEM((64, 8, 128), BF16), pltpu.VMEM((64, 128), F32),
-            dma((11,)), dma((4,)), dma((4,)), dma((8,)), dma((8,)), dma((8,)), dma((8,)), dma((15,)), dma((15,)), dma((15,)),
+            dma((11,)), dma((16,)), dma((16,)), dma((8,)), dma((8,)), dma((8,)), dma((8,)), dma((15,)), dma((15,)), dma((15,)),
             dma((15,)), dma((15,)), dma((15,)), dma((64,)), dma((64,)), dma((32,)), dma((32,)), dma((32,)), dma((32,)),
             pltpu.SemaphoreType.REGULAR, pltpu.SemaphoreType.REGULAR,
         ],
@@ -348,7 +330,9 @@
 
 def hand_over(*refs):
     sems = refs[-1]
-    copies = [pltpu.make_async_copy(refs[k], refs[5 + k], sems.at[k]) for k in (4, 0, 1, 2, 3)]
+    pairs = [(refs[4].at[pl.ds(16 * k, 16)], refs[9].at[pl.ds(16 * k, 16)]) for k in range(4)]
+    pairs += [(refs[k], refs[5 + k]) for k in range(4)]
+    copies = [pltpu.make_async_copy(a, b, sems.at[k]) for k, (a, b) in enumerate(pairs)]
     for c in copies:
         c.start()
     for c in copies:
@@ -372,7 +356,7 @@
         out_shape=tuple(jax.ShapeDtypeStruct(o.shape, o.dtype) for o in outs),
         in_specs=[pl.BlockSpec(memory_space=pltpu.VMEM)] * 5,
         out_specs=(pl.BlockSpec(memory_space=pltpu.HBM),) * 5,
-        scratch_shapes=[pltpu.SemaphoreType.DMA((5,))],
+        scratch_shapes=[pltpu.SemaphoreType.DMA((8,))],
         name="hand_over",
     )(*(pltpu.with_memory_space_constraint(o, pltpu.VMEM) for o in outs))
     return from_flat(a), from_flat(b), from_flat(c)[None], from_flat(d)[None], model

time: 53.9 us -> 53 us (0.983)
  Pallas kernels: 52.4 us -> 51.6 us
    pallas_call x1, Pallas kernels: 51.4 us -> 50.4 us  [outer_step(): pl.pallas_call(kernel, out_shape=(out, out, out, out, pltpu.VMEM((64, 819...]
where the time goes in v5:
time: 53 us; the launch traced here: 52.8 us
  Pallas kernels  51.6 us (97%)
  between operations  1.29 us (2%)
    pallas_call x1, Pallas kernels, outer_step(): pl.pallas_call(kernel, out_shape=(out, out, out, out, pltpu.VMEM((64, 819...  50.4 us
    pallas_call x1, Pallas kernels, on_device(): pl.pallas_call(hand_over, out_shape=tuple((jax.ShapeDtypeStruct(o.shape,...  1.11 us

profile of v5, /device:TPU:1, one launch (start us, length us, event | category | flops | bytes accessed | tf_op | source)
XLA Modules:
  0.0 52.8 jit_solution(17008753480448936405)
XLA Ops:
  1.3 50.4 %outer_step.1 = (f32[128,128]{1,0:T(8,128)S(1)}, f32[128,128]{1,0:T(8,128)S(1)}, f32[128,128]{1,0:T(8,128)S(1)}, f32[128,128]{1,0:T(8,128)S(1)}, bf16[64,8192]{1,0:T(8,128)(2,1)S(1)}) custom-call(bf16[64,8192]{1,0:T(8,128)(2,1)} %bitcast.46, f32[128,128]{1,0:T(8,128)} %bitcast.47, f32[128,128]{1,0:T(8,128)} %bitcast.48, f32[128,128]{1,0:T(8,128)} %bitcast.49, ...), custom_call_target="tpu_custom_call" | custom-call | tf_op jit(solution)/shard_map/outer_step/pallas_call | solution.py:308
  51.7 1.1 %hand_over.1 = (f32[128,128]{1,0:T(8,128)}, f32[128,128]{1,0:T(8,128)}, f32[128,128]{1,0:T(8,128)}, f32[128,128]{1,0:T(8,128)}, bf16[64,8192]{1,0:T(8,128)(2,1)}) custom-call(f32[128,128]{1,0:T(8,128)S(1)} %get-tuple-element.15.refs_0_, f32[128,128]{1,0:T(8,128)S(1)} %get-tuple-element.16.refs_1_, f32[128,128]{1,0:T(8,128)S(1)} %get-tuple-element.17.refs_2_, ...), custom_call_target="tpu_custom_call" | custom-call | tf_op jit(solution)/shard_map/hand_over/pallas_call | solution.py:354

commit v6 on v5

--- a/solution.py
+++ b/solution.py
@@ -32,7 +32,6 @@
     other = 1 - core
     zs = [lax.rem(z + d, 8) for d in range(8)]
     ys = [lax.rem(y + d, 8) * 2 for d in range(8)]
-    back_ys = [lax.rem(y + 8 - d, 8) * 2 for d in range(8)]
     xls = [xl, 1 - xl]
 
     def at(px, pz, pc):
@@ -44,6 +43,12 @@
         return pltpu.make_async_remote_copy(
             source, target, send, recv, device_id=device, device_id_type=MESH
         )
+
+    def all_sent(ref, sem):
+        remote(ref, ref, sem.at[0], sem.at[0], sibling).wait_send()
+
+    def all_arrived(ref, sem):
+        remote(ref, ref, sem, sem, sibling).wait_recv()
 
     barrier = pltpu.get_barrier_semaphore()
 
@@ -71,6 +76,18 @@
     ]
     for c in loads + small:
         c.start()
+    for d in RING[:7]:
+        greet(at(xh, zs[d], 1))
+    for dy, dx in PEERS:
+        greet((ys[dy] + xls[dx], f + 1 - core))
+
+    def tell(sem):
+        pl.semaphore_signal(sem, inc=1, device_id=sibling, device_id_type=MESH)
+
+    @pl.when(core == 0)
+    def _():
+        pl.semaphore_wait(barrier, 3)
+        tell(near)
 
     def regroup(k):
         loads[k].wait()
@@ -89,33 +106,23 @@
                         BF16
                     )
 
-    for k in range(4):
-        regroup(k)
-
     chips = [(1 - xh) * 8 + zs[d] for d in RING] + [xh * 8 + zs[d] for d in RING]
     swaps = [
-        remote(by_owner.at[other, chip], sib.at[k], s_sib.at[k], r_sib.at[k], sibling)
+        remote(by_owner.at[other, chip], sib.at[k], s_sib.at[0], r_sib.at[k], sibling)
         for k, chip in enumerate(chips)
     ]
 
-    def tell(sem):
-        pl.semaphore_signal(sem, inc=1, device_id=sibling, device_id_type=MESH)
-
-    @pl.when(core == 0)
-    def _():
-        pl.semaphore_wait(barrier, 3)
-        tell(near)
+    regroup(0)
+    regroup(1)
 
     @pl.when(core == 1)
     def _():
         pl.semaphore_wait(near, 1)
 
-    for c in swaps:
-        c.start()
-    for d in RING[:7]:
-        greet(at(xh, zs[d], 1))
-    for dy, dx in PEERS:
-        greet((ys[dy] + xls[dx], f + 1 - core))
+    for c in swaps[:8]:
+        c.start()
+    regroup(2)
+    regroup(3)
 
     def pair(k):
         swaps[k].wait_recv()
@@ -127,9 +134,10 @@
     crossing = []
     for k, d in enumerate(RING):
         cross_code[d] = to_codes(pair(k) * CODE)
-        c = remote(cross_code.at[d], x_code.at[d], s_x.at[d], r_x.at[d], across_x)
+        c = remote(cross_code.at[d], x_code.at[d], s_x.at[0], r_x.at[d], across_x)
         c.start()
         crossing.append(c)
+        swaps[8 + k].start()
 
     for c in small[:4]:
         c.wait()
@@ -163,15 +171,14 @@
         both = own + x_code[d].astype(F32)
         if d:
             out_code[d] = to_codes(0.5 * both)
-            c = remote(out_code.at[d], in_code.at[d], s_code.at[d], r_code.at[d], at(xh, zs[d], core))
+            c = remote(out_code.at[d], in_code.at[d], s_code.at[0], r_code.at[d], at(xh, zs[d], core))
             c.start()
             along.append(c)
     kept = both * (1.0 / CODE)
 
     group_at = [(ys[dy] + xls[dx], xls[dx] * 8 + ys[dy] // 2) for dy, dx in PEERS]
-    group_from = [xls[dx] * 8 + back_ys[dy] // 2 for dy, dx in PEERS]
     own_eight = xl * 8 + y
-    w_copies = [remote(w_out, w_in.at[i], s_w.at[i], r_w.at[i], (p, f)) for i, (p, _) in enumerate(group_at)]
+    w_copies = [remote(w_out, w_in.at[i], s_w.at[0], r_w.at[0], (p, f)) for i, (p, _) in enumerate(group_at)]
     for c in w_copies:
         c.start()
 
@@ -198,7 +205,7 @@
         return pl.ds(pl.multiple_of(p * 8, 8), 8)
 
     part_copies = [
-        remote(weighted.at[eight(e)], part.at[i], s_part.at[i], r_part.at[i], (p, f))
+        remote(weighted.at[eight(e)], part.at[i], s_part.at[0], r_part.at[0], (p, f))
         for i, (p, e) in enumerate(group_at)
     ]
     for c in part_copies:
@@ -206,12 +213,12 @@
     o_m[...] = moment
     o_s[...] = second
     all_weights = w_out[...]
+    all_arrived(w_in, r_w.at[0])
     for i in range(15):
-        w_copies[i].wait_recv()
         all_weights = all_weights + w_in[i]
     own_sum = weighted[eight(own_eight), :]
+    all_arrived(part, r_part.at[0])
     for i in range(15):
-        part_copies[i].wait_recv()
         own_sum = own_sum + part[i]
     own_mean = own_sum / all_weights
 
@@ -228,19 +235,19 @@
     slice_copies = []
     for n, (dy, dz) in enumerate(PLANE + ((0, 0),)):
         to = (ys[dy] + xl, xh * 16 + zs[dz] * 2 + z_half)
-        copy = remote(slice_out.at[0], slice_in.at[where], s_slice.at[n], r_slice.at[where], to)
+        copy = remote(slice_out.at[0], slice_in.at[where], s_slice.at[0], r_slice.at[y], to)
         slice_copies.append(copy)
         if n < 63:
             copy.start()
         else:
             pl.when(z_half != core)(copy.start)
-            keep = pltpu.make_async_copy(slice_out.at[0], slice_in.at[where], r_slice.at[where])
+            keep = pltpu.make_async_copy(slice_out.at[0], slice_in.at[where], r_slice.at[y])
             pl.when(z_half == core)(keep.start)
 
     mean_copies = []
     own_rows = mean.at[eight(own_eight)]
     for i, (p, _) in enumerate(group_at):
-        c = remote(own_rows, own_rows, s_mean.at[i], r_mean.at[i], (p, f))
+        c = remote(own_rows, own_rows, s_mean.at[0], r_mean.at[0], (p, f))
         c.start()
         mean_copies.append(c)
 
@@ -252,13 +259,11 @@
         column = (lax.rem(source_x, 2) * 8 + ys[d] // 2) * 512
         return o_model.at[pl.ds(pl.multiple_of(row, 16), 16), pl.ds(pl.multiple_of(column, 512), 512)]
 
-    sends = []
     for n, d in enumerate(reversed(RING)):
         from_y = ys[d] // 2
-        for k in range(8):
-            slot = from_y * 8 + k
-            remote(slice_out.at[0], slice_in.at[slot], s_slice.at[0], r_slice.at[slot], sibling).wait_recv()
-        arrived = slice_in[pl.ds(pl.multiple_of(from_y * 8, 8), 8)].astype(F32)
+        slots = pl.ds(pl.multiple_of(from_y * 8, 8), 8)
+        all_arrived(slice_in.at[slots], r_slice.at[from_y])
+        arrived = slice_in[slots].astype(F32)
         sorted_rows[...] = arrived.reshape(64, 128)
         piece = block(x, core, d)
         for j in range(4):
@@ -266,34 +271,33 @@
             piece[:, j * 128 : j * 128 + 128] = jnp.concatenate(two, axis=0).astype(BF16)
         for dx in CROSS:
             to = (y * 2 + lax.rem(xs[dx], 2), xs[dx] // 2 * 16 + z * 2 + core)
-            sends.append(remote(piece, piece, s_block.at[dx * 8 + n], r_block.at[dx * 8 + n], to))
-            sends[-1].start()
-        sends.append(remote(piece, piece, s_fwd.at[n], r_fwd.at[n], sibling))
-        sends[-1].start()
-
-    for i, e in enumerate(group_from):
-        remote(mean.at[eight(e)], mean.at[eight(e)], s_mean.at[i], r_mean.at[i], sibling).wait_recv()
+            remote(piece, piece, s_block.at[0], r_block.at[dx * 8 + n], to).start()
+        remote(piece, piece, s_fwd.at[0], r_fwd.at[0], sibling).start()
+
+    fifteen = mean.at[pl.ds(0, 120)]
+    all_arrived(fifteen, r_mean.at[0])
     everything = pl.ds(0, 128)
     o_master[...], o_mom[...] = nesterov(everything, mean[...])
 
-    for c in swaps + crossing + along + w_copies + part_copies + mean_copies + slice_copies[:63]:
-        c.wait_send()
+    all_sent(sib, s_sib)
+    all_sent(cross_code, s_x)
+    all_sent(out_code.at[pl.ds(0, 7)], s_code)
+    all_sent(w_in, s_w)
+    all_sent(part, s_part)
+    all_sent(fifteen, s_mean)
+    all_sent(slice_in.at[pl.ds(0, 63)], s_slice)
     pl.when(z_half != core)(slice_copies[63].wait_send)
 
     for n, d in enumerate(reversed(RING)):
         for dx in CROSS:
             piece = block(xs[4 - dx], core, d)
             at_n = dx * 8 + n
-            remote(piece, piece, s_block.at[at_n], r_block.at[at_n], sibling).wait_recv()
-            sends.append(remote(piece, piece, s_fwd.at[at_n], r_fwd.at[at_n], sibling))
-            sends[-1].start()
-    for n, d in enumerate(reversed(RING)):
-        for dx in (0,) + CROSS:
-            piece = block(xs[(4 - dx) % 4], other, d)
-            at_n = dx * 8 + n
-            remote(piece, piece, s_fwd.at[at_n], r_fwd.at[at_n], sibling).wait_recv()
-    for c in sends:
-        c.wait_send()
+            remote(piece, piece, s_block.at[0], r_block.at[at_n], sibling).wait_recv()
+            remote(piece, piece, s_fwd.at[0], r_fwd.at[0], sibling).start()
+    all_sent(o_model.at[pl.ds(0, 48), pl.ds(0, 4096)], s_block)
+    rows_32 = o_model.at[pl.ds(0, 32)]
+    all_arrived(rows_32, r_fwd.at[0])
+    all_sent(rows_32, s_fwd)
 
 
 def outer_step(*args):
@@ -304,6 +308,7 @@
     codes16 = pltpu.VMEM((8, 128, 128), jnp.int16)
     eight = lambda n: pltpu.VMEM((n, 8, 128), F32)
     dma = pltpu.SemaphoreType.DMA
+    one = dma((1,))
     out = pltpu.VMEM((128, 128), F32)
     return pl.pallas_call(
         kernel,
@@ -317,8 +322,8 @@
             square, square, square, square, eight(15), square,
             pltpu.VMEM((8, 128), F32), eight(15), pltpu.VMEM((8, 128), F32),
             pltpu.VMEM((1, 8, 128), BF16), pltpu.VMEM((64, 8, 128), BF16), pltpu.VMEM((64, 128), F32),
-            dma((11,)), dma((16,)), dma((16,)), dma((8,)), dma((8,)), dma((8,)), dma((8,)), dma((15,)), dma((15,)), dma((15,)),
-            dma((15,)), dma((15,)), dma((15,)), dma((64,)), dma((64,)), dma((32,)), dma((32,)), dma((32,)), dma((32,)),
+            dma((11,)), one, dma((16,)), one, dma((8,)), one, dma((8,)), one, one, one, one, one, one, one, dma((8,)),
+            one, dma((32,)), one, one,
             pltpu.SemaphoreType.REGULAR, pltpu.SemaphoreType.REGULAR,
         ],
         compiler_params=pltpu.CompilerParams(

time: 53 us -> 50.5 us (0.953)
  Pallas kernels: 51.6 us -> 49 us
    pallas_call x1, Pallas kernels: 50.4 us -> 47.9 us  [outer_step(): pl.pallas_call(kernel, out_shape=(out, out, out, out, pltpu.VMEM((64, 819...]
where the time goes in v6:
time: 50.5 us; the launch traced here: 50.3 us
  Pallas kernels  49 us (97%)
  between operations  1.29 us (3%)
    pallas_call x1, Pallas kernels, outer_step(): pl.pallas_call(kernel, out_shape=(out, out, out, out, pltpu.VMEM((64, 819...  47.9 us
    pallas_call x1, Pallas kernels, on_device(): pl.pallas_call(hand_over, out_shape=tuple((jax.ShapeDtypeStruct(o.shape,...  1.11 us

profile of v6, /device:TPU:1, one launch (start us, length us, event | category | flops | bytes accessed | tf_op | source)
XLA Modules:
  0.0 50.3 jit_solution(3835349755115344258)
XLA Ops:
  1.3 47.9 %outer_step.1 = (f32[128,128]{1,0:T(8,128)S(1)}, f32[128,128]{1,0:T(8,128)S(1)}, f32[128,128]{1,0:T(8,128)S(1)}, f32[128,128]{1,0:T(8,128)S(1)}, bf16[64,8192]{1,0:T(8,128)(2,1)S(1)}) custom-call(bf16[64,8192]{1,0:T(8,128)(2,1)} %bitcast.46, f32[128,128]{1,0:T(8,128)} %bitcast.47, f32[128,128]{1,0:T(8,128)} %bitcast.48, f32[128,128]{1,0:T(8,128)} %bitcast.49, ...), custom_call_target="tpu_custom_call" | custom-call | tf_op jit(solution)/shard_map/outer_step/pallas_call | solution.py:313
  49.2 1.1 %hand_over.1 = (f32[128,128]{1,0:T(8,128)}, f32[128,128]{1,0:T(8,128)}, f32[128,128]{1,0:T(8,128)}, f32[128,128]{1,0:T(8,128)}, bf16[64,8192]{1,0:T(8,128)(2,1)}) custom-call(f32[128,128]{1,0:T(8,128)S(1)} %get-tuple-element.15.refs_0_, f32[128,128]{1,0:T(8,128)S(1)} %get-tuple-element.16.refs_1_, f32[128,128]{1,0:T(8,128)S(1)} %get-tuple-element.17.refs_2_, ...), custom_call_target="tpu_custom_call" | custom-call | tf_op jit(solution)/shard_map/hand_over/pallas_call | solution.py:359
